TPU v7x, 128 devices: a whole 4x4x4 slice. The times are simulated.
128 devices in a mesh: lat: 32 (over z, y_hi, x), lon: 4 (over y_lo, core).
Axes of the slice: x: 4, y: 4 (y_hi: 2, y_lo: 2; y = y_hi * 2 + y_lo), z: 4, core: 2. Of those that a mesh axis runs over, the one named last changes fastest.
Arguments:
- level_tokens: bfloat16 [256, 64, 13, 1024], P(('lat', 'lon')), may hold values from -24 to 24
- latent_query: bfloat16 [3, 1024], replicated, may hold values from -6 to 6
- key_weight: bfloat16 [1024, 1024], replicated, may hold values from -0.1875 to 0.1875
- value_weight: bfloat16 [1024, 1024], replicated, may hold values from -0.1875 to 0.1875
- resample_out: bfloat16 [1024, 1024], replicated, may hold values from -0.1875 to 0.1875
- norm_gain: float32 [2, 1024], replicated, may hold values from 0.5 to 1.5
- qkv_weight: bfloat16 [2, 1024, 3, 1024], P(None, 'lat', None, 'lon'), may hold values from -0.1875 to 0.1875
- out_weight: bfloat16 [2, 1024, 1024], P(None, 'lat', 'lon'), may hold values from -0.1875 to 0.1875
- window_label: int32 [256, 64], P('lat', 'lon'), may hold values from 0 to 3
- grad_latents: bfloat16 [256, 64, 3, 1024], P(('lat', 'lon')), may hold values from -6 to 6
Outputs:
- backbone_out: bfloat16 [256, 64, 3, 1024], P('lat', 'lon')
- grad_key_weight: float32 [1024, 1024], P(('lat', 'lon'))
- grad_value_weight: float32 [1024, 1024], P(('lat', 'lon'))
- grad_out_weight: float32 [1024, 1024], P(('lat', 'lon'))
All inputs are finite; a program needn't handle non-finite values.
Results may differ from a plain program's by a relative error of at most 0.013.
Values may be sent and summed in bfloat16 or wider, within the bound.
A program may use at most 192 MiB of HBM per device.

v0:
```python
import jax
import jax.numpy as jnp
from jax import lax
from jax.sharding import PartitionSpec as P

HEADS = 16


def from_behind(block, axis, distance):
    devices = range(lax.axis_size(axis))
    route = [((i - distance) % len(devices), i) for i in devices]
    return lax.ppermute(block, axis, route)


def layer_norm(stream, norm_scale):
    values = stream.astype(jnp.float32)
    centre = jnp.mean(values, axis=-1, keepdims=True)
    centred = values - centre
    spread = jnp.mean(centred * centred, axis=-1, keepdims=True)
    return (centred * lax.rsqrt(spread + 1e-05) * norm_scale).astype(jnp.bfloat16)


def to_windows(stream):
    tile_rows, tile_cols, levels = (stream.shape[0], stream.shape[1], stream.shape[2])
    trailing = stream.shape[3:]
    window_grid = stream.reshape((tile_rows // 4, 4, tile_cols // 8, 8, levels) + trailing)
    window_grid = jnp.swapaxes(window_grid, 1, 2)
    return window_grid.reshape((tile_rows // 4 * (tile_cols // 8), 32 * levels) + trailing)


def from_windows(windowed, tile_rows, tile_cols):
    levels = windowed.shape[1] // 32
    trailing = windowed.shape[2:]
    window_grid = windowed.reshape((tile_rows // 4, tile_cols // 8, 4, 8, levels) + trailing)
    window_grid = jnp.swapaxes(window_grid, 1, 2)
    return window_grid.reshape((tile_rows, tile_cols, levels) + trailing)


def window_attend(projected, window_codes):
    head_size = projected.shape[-1]
    logits = jnp.einsum(
        "wqhe,wkhe->whqk",
        projected[:, :, 0],
        projected[:, :, 1],
        preferred_element_type=jnp.float32,
    ) * head_size ** (-0.5)
    allowed = window_codes[:, None, :, None] == window_codes[:, None, None, :]
    logits = jnp.where(allowed, logits, -1e30)
    weights = jax.nn.softmax(logits, axis=-1).astype(jnp.bfloat16)
    attended = jnp.einsum(
        "whqk,wkhe->wqhe", weights, projected[:, :, 2], preferred_element_type=jnp.float32
    )
    return attended.astype(jnp.bfloat16).reshape(projected.shape[0], projected.shape[1], -1)


def resample(level_tokens, latent_query, key_weight, value_weight, resample_out, grad_latents):
    stripe_rows, lon_cells, levels, model_width = level_tokens.shape
    latent = latent_query.shape[0]
    head_size = model_width // HEADS
    score_scale = head_size ** (-0.5)
    patch_count = stripe_rows * lon_cells
    flat_tokens = level_tokens.reshape(-1, model_width)
    level_keys = jnp.dot(flat_tokens, key_weight, preferred_element_type=jnp.float32).astype(
        jnp.bfloat16
    )
    level_values = jnp.dot(flat_tokens, value_weight, preferred_element_type=jnp.float32).astype(
        jnp.bfloat16
    )
    key_heads = level_keys.reshape(patch_count, levels, HEADS, head_size)
    value_heads = level_values.reshape(patch_count, levels, HEADS, head_size)
    query_heads = latent_query.reshape(latent, HEADS, head_size)
    logits = (
        jnp.einsum("qhe,plhe->phql", query_heads, key_heads, preferred_element_type=jnp.float32)
        * score_scale
    )
    level_probs = jax.nn.softmax(logits, axis=-1)
    level_weights = level_probs.astype(jnp.bfloat16)
    attended = jnp.einsum(
        "phql,plhe->pqhe", level_weights, value_heads, preferred_element_type=jnp.float32
    ).astype(jnp.bfloat16)
    attended_flat = attended.reshape(-1, model_width)
    latents = jnp.dot(attended_flat, resample_out, preferred_element_type=jnp.float32).reshape(
        patch_count, latent, model_width
    )
    latents = (latents + latent_query.astype(jnp.float32)[None]).astype(jnp.bfloat16)
    grad_flat = grad_latents.reshape(-1, model_width)
    d_attended = lax.dot_general(
        grad_flat, resample_out, (((1,), (1,)), ((), ())), preferred_element_type=jnp.float32
    )
    d_attended = d_attended.astype(jnp.bfloat16).reshape(patch_count, latent, HEADS, head_size)
    d_weights = jnp.einsum(
        "pqhe,plhe->phql", d_attended, value_heads, preferred_element_type=jnp.float32
    )
    d_logits = level_probs * (d_weights - jnp.sum(level_probs * d_weights, axis=-1, keepdims=True))
    d_values = jnp.einsum(
        "phql,pqhe->plhe", level_weights, d_attended, preferred_element_type=jnp.float32
    )
    d_values = d_values.astype(jnp.bfloat16).reshape(-1, model_width)
    d_keys = jnp.einsum("phql,qhe->plhe", d_logits, query_heads.astype(jnp.float32)) * score_scale
    d_keys = d_keys.astype(jnp.bfloat16).reshape(-1, model_width)
    return (
        latents.reshape(stripe_rows, lon_cells, latent, model_width),
        flat_tokens,
        d_keys,
        d_values,
        attended_flat,
        grad_flat,
    )


def sublayer(stream, token_codes, layer_index, norm_gain, qkv_weight, out_weight):
    tile_rows, tile_cols, latent, model_width = stream.shape
    head_size = model_width // HEADS
    normed = layer_norm(stream, norm_gain[layer_index])
    window_count = tile_rows // 4 * (tile_cols // 8)
    window_size = 32 * latent
    weight_shard = qkv_weight[layer_index]
    wide_weight = lax.all_gather(weight_shard, "lon", axis=2, tiled=True)
    tile_flat = to_windows(normed).reshape(-1, model_width)
    weight_piece = lax.all_gather(wide_weight, "lat", axis=0, tiled=True)
    projected = jnp.dot(
        tile_flat,
        weight_piece.reshape(weight_piece.shape[0], -1),
        preferred_element_type=jnp.float32,
    )
    projected = projected.astype(jnp.bfloat16).reshape(
        window_count, window_size, 3, HEADS, head_size
    )
    attended = window_attend(projected, to_windows(token_codes)).reshape(-1, model_width)
    wide_out = lax.all_gather(out_weight[layer_index], "lon", axis=1, tiled=True)
    update = jnp.dot(
        attended,
        lax.all_gather(wide_out, "lat", axis=0, tiled=True),
        preferred_element_type=jnp.float32,
    )
    update = from_windows(
        update.reshape(window_count, window_size, model_width), tile_rows, tile_cols
    )
    return (stream.astype(jnp.float32) + update).astype(jnp.bfloat16)


def local(
    level_tokens,
    latent_query,
    key_weight,
    value_weight,
    resample_out,
    norm_gain,
    qkv_weight,
    out_weight,
    window_label,
    grad_latents,
):
    lat_devices = lax.axis_size("lat")
    lon_devices = lax.axis_size("lon")
    stripe_rows, lon_cells = (level_tokens.shape[0], level_tokens.shape[1])
    latent, model_width = latent_query.shape
    stripe_latents, flat_tokens, d_keys, d_values, attended_flat, grad_flat = resample(
        level_tokens, latent_query, key_weight, value_weight, resample_out, grad_latents
    )
    factor = (stripe_rows * lon_cells * lat_devices * lon_devices) ** (-0.5)
    contract_rows = (((0,), (0,)), ((), ()))
    grad_key = lax.dot_general(
        flat_tokens, d_keys, contract_rows, preferred_element_type=jnp.float32
    )
    grad_value = lax.dot_general(
        flat_tokens, d_values, contract_rows, preferred_element_type=jnp.float32
    )
    grad_out = lax.dot_general(
        attended_flat, grad_flat, contract_rows, preferred_element_type=jnp.float32
    )
    grad_key, grad_value, grad_out = (
        lax.psum_scatter(grad_key * factor, ("lat", "lon"), scatter_dimension=0, tiled=True),
        lax.psum_scatter(grad_value * factor, ("lat", "lon"), scatter_dimension=0, tiled=True),
        lax.psum_scatter(grad_out * factor, ("lat", "lon"), scatter_dimension=0, tiled=True),
    )
    tile_rows = stripe_rows * lon_devices
    tile_cols = lon_cells // lon_devices
    split_latents = stripe_latents.reshape(stripe_rows, lon_devices, tile_cols, latent, model_width)
    tiles = lax.all_to_all(split_latents, "lon", split_axis=1, concat_axis=0, tiled=True).reshape(
        tile_rows, tile_cols, latent, model_width
    )
    plain = jnp.zeros((tile_rows, tile_cols, latent), jnp.float32)
    middle = sublayer(tiles, plain, 0, norm_gain, qkv_weight, out_weight)
    edge_rows = from_behind(middle[:2], "lat", -1)
    shifted = jnp.concatenate([middle[2:], edge_rows], axis=0)
    edge_cols = from_behind(shifted[:, :4], "lon", -1)
    rolled = jnp.concatenate([shifted[:, 4:], edge_cols], axis=1)
    row_index = lax.axis_index("lat") * tile_rows + jnp.arange(tile_rows, dtype=jnp.int32)
    wrapped = (row_index >= tile_rows * lat_devices - 2).astype(jnp.int32)
    token_codes = (window_label * 2 + wrapped[:, None]).astype(jnp.float32)
    token_codes = jnp.broadcast_to(token_codes[:, :, None], (tile_rows, tile_cols, latent))
    backbone_out = sublayer(rolled, token_codes, 1, norm_gain, qkv_weight, out_weight)
    return (backbone_out, grad_key, grad_value, grad_out)


def solution(mesh):
    in_specs = (
        P(("lat", "lon"), None, None, None),
        P(),
        P(),
        P(),
        P(),
        P(),
        P(None, "lat", None, "lon"),
        P(None, "lat", "lon"),
        P("lat", "lon"),
        P(("lat", "lon"), None, None, None),
    )
    out_specs = (
        P("lat", "lon", None, None),
        P(("lat", "lon"), None),
        P(("lat", "lon"), None),
        P(("lat", "lon"), None),
    )
    return jax.shard_map(local, mesh=mesh, in_specs=in_specs, out_specs=out_specs, check_vma=False)
```

profile of v0, /device:TPU:1, one launch (start us, length us, event | category | flops | bytes accessed | tf_op | source)
XLA Modules:
  0.0 2089.9 jit_solution(10596605034681778668)
XLA Ops:
  9.0 7.3 all-gather
  17.2 5.8 all-gather.2
  23.0 6.1 all-gather.4
  29.2 5.8 all-gather.6
  35.0 5.9 copy.137
  40.9 6.1 reshape.164
  47.0 7.1 convolution_convert_fusion.2
  54.1 9.8 reshape.166
  64.0 7.1 convolution_convert_fusion.3
  71.1 9.8 reshape.165
  86.8 9.4 fusion.2
  100.4 6.8 fusion.85
  110.5 11.4 copy.181
  121.9 9.9 reshape.176
  131.8 9.1 multiply_bitcast_fusion.1
  140.9 5.4 copy.201
  149.3 5.9 convert_bitcast_fusion.1
  180.7 6.2 copy.184
  186.9 9.9 reshape.177
  196.8 9.0 multiply_bitcast_fusion
  214.7 8.6 copy.150
  223.3 8.6 convolution_convert_fusion.1
  231.9 6.7 reshape.206
  238.6 5.6 fusion.81
  269.1 7.9 collective-permute-start
  282.6 8.9 copy.165
  298.0 8.3 convolution_convert_fusion
  306.3 6.7 reshape.207
  336.5 9.3 all-gather.19.cloned.1.call-done
  350.1 450.6 %reduce-scatter.10.cloned.1.call-done = f32[8,1024]{1,0:T(8,128)} async-done(((f32[1024,1024]{1,0:T(8,128)}), f32[8,1024]{1,0:T(8,128)}) %reduce-scatter.10.cloned.1.call-update) | async-done | bytes 32784
  800.7 640.8 %reduce-scatter.8.cloned.1.call-done = f32[8,1024]{1,0:T(8,128)} async-done(((f32[1024,1024]{1,0:T(8,128)}), f32[8,1024]{1,0:T(8,128)}) %reduce-scatter.8.cloned.1.call-update) | async-done | bytes 32784 | tf_op jit(solution)/shard_map/reduce_scatter | solution.py:175
  1441.5 640.7 %reduce-scatter.12.cloned.1.call-done = f32[8,1024]{1,0:T(8,128)} async-done(((f32[1024,1024]{1,0:T(8,128)}), f32[8,1024]{1,0:T(8,128)}) %reduce-scatter.12.cloned.1.call-update) | async-done | bytes 32784
  (124 shorter events, 117.2 us)
Async XLA Ops:
  8.0 39.0 %copy-start = (bf16[1024,1024]{1,0:T(8,128)(2,1)S(1)}, bf16[1024,1024]{1,0:T(8,128)(2,1)}, u32[]{:S(2)}) copy-start(bf16[1024,1024]{1,0:T(8,128)(2,1)} %param.12) | copy-start | bytes 6291460
  8.0 206.6 %all-gather.13.cloned.1.call-start = ((), (), s32[]{:S(2)}) async-start(), calls=%async_computation.5 | async-start | bytes 6488064 | tf_op jit(solution)/shard_map/all_gather | solution.py:120
  16.4 248.5 %all-gather.15.cloned.1.call-start = ((), (), s32[]{:S(2)}) async-start(), calls=%async_computation.6 | async-start | bytes 2162688 | tf_op jit(solution)/shard_map/all_gather | solution.py:133
  23.0 259.6 %all-gather.17.cloned.1.call-start = ((), (), s32[]{:S(2)}) async-start(), calls=%async_computation.7 | async-start | bytes 6488064 | tf_op jit(solution)/shard_map/all_gather | solution.py:120
  29.1 316.6 %all-gather.19.cloned.1.call-start = ((), (), s32[]{:S(2)}) async-start(), calls=%async_computation.8 | async-start | bytes 2162688 | tf_op jit(solution)/shard_map/all_gather | solution.py:133
  35.0 765.7 %reduce-scatter.10.cloned.1.call-start = ((), (), s32[]{:S(2)}) async-start(), calls=%async_computation.9 | async-start | bytes 4227072
  54.1 9.8 copy-start.8
  54.1 9.9 copy-start.11
  71.1 9.8 copy-start.7
  82.2 0.9 copy-start.4
  146.3 1295.2 %reduce-scatter.8.cloned.1.call-start = ((), (), s32[]{:S(2)}) async-start(), calls=%async_computation.4 | async-start | bytes 4227072 | tf_op jit(solution)/shard_map/reduce_scatter | solution.py:175
  155.2 1.3 copy-start.2
  172.1 39.9 %all-to-all-start = ((bf16[2,4,16,3,1024]{4,2,3,0,1:T(8,128)(2,1)}), bf16[2,4,16,3,1024]{4,2,3,0,1:T(8,128)(2,1)S(1)}, u32[]{:S(2)}, u32[]{:S(2)}) async-start(bf16[2,4,16,3,1024]{4,2,3,0,1:T(8,128)(2,1)} %copy.144), calls=%async_computation | async-start | bytes 1572864 | tf_op jit(solution)/shard_map/all_to_all | solution.py:180
  175.8 1906.4 %reduce-scatter.12.cloned.1.call-start = ((), (), s32[]{:S(2)}) async-start(), calls=%async_computation.10 | async-start | bytes 4227072
  211.1 0.7 copy-start.10
  211.1 0.8 copy-start.9
  254.7 3.7 copy-start.6
  268.2 0.9 copy-start.3
  269.1 12.1 collective-permute-start
  281.3 10.4 collective-permute-start.1
  328.6 1.2 copy-start.5
  345.7 1736.4 %copy-start.1 = (bf16[1024,1024]{1,0:T(8,128)(2,1)S(1)}, bf16[1024,1024]{1,0:T(8,128)(2,1)}, u32[]{:S(2)}) copy-start(bf16[1024,1024]{1,0:T(8,128)(2,1)} %param.12) | copy-start | bytes 6291460
Sparse Core Ops, SparseCore 0:
  16.5 93.7 all-gather.12
  113.2 67.6 all-gather.14
  184.0 91.3 all-gather.16
  278.2 67.4 all-gather.18
Sparse Core Ops, SparseCore 1:
  146.4 654.3 reduce-scatter.9
  803.6 637.8 reduce-scatter.7
  1444.3 637.8 reduce-scatter.11
where the time goes:
time: 2100 us; the launch traced here: 2090 us
  waiting for transfers between devices  1740 us (83%)
  local copies, waits for them, and re-layouts  178 us (8%)
  matrix products  102 us (5%)
  blocking collectives  25 us (1%)
    unnamed x9, waiting for transfers between devices  1090 us
    reduce_scatter x1, waiting for transfers between devices, local(): lax.psum_scatter(grad_out * factor, ('lat', 'lon'), scatter_dimension=0,...  641 us
  transfers between devices with their start and end apart: 10, of which 5 were waited for; matrix products, arithmetic and copies ran while one was open for 14% of the time, Pallas kernels for 0%

commit v1 on v0

v1 whole, which is shorter than its diff:
```python
import functools

import jax
import jax.numpy as jnp
from jax import lax
from jax.experimental import pallas as pl
from jax.experimental.pallas import tpu as pltpu
from jax.sharding import PartitionSpec as P

MESH = pl.DeviceIdType.MESH
F32, BF16 = jnp.float32, jnp.bfloat16
D = 1024
HEADS = 16
LEV = 13
LATENT = 3
GROUPS = 8
MIB = 1024 * 1024
PACK = 512
ORDERS = (("x", "y", "z"), ("y", "z", "x"), ("z", "x", "y"))


def dot(a, b, dims=((1,), (0,))):
    return lax.dot_general(a, b, (dims, ((), ())), preferred_element_type=F32)


def my_place():
    lat, lon = lax.axis_index("lat"), lax.axis_index("lon")
    return {
        "z": lat // 8,
        "y": ((lat // 4) % 2) * 2 + lon // 2,
        "x": lat % 4,
        "core": lon % 2,
    }


def device_of(place):
    lat = place["z"] * 8 + (place["y"] // 2) * 4 + place["x"]
    return (lat, (place["y"] % 2) * 2 + place["core"])


def moved(place, dim, delta):
    size = 2 if dim == "core" else 4
    other = dict(place)
    other[dim] = (place[dim] + delta + size) % size
    return device_of(other)


def pick(dim, value):
    if dim == "y":
        if value is None:
            return {"yh": slice(None), "yl": slice(None)}
        return {"yh": pl.ds(value // 2, 1), "yl": pl.ds(value % 2, 1)}
    return {dim: slice(None) if value is None else pl.ds(value, 1)}


def greet(place):
    barrier = pltpu.get_barrier_semaphore()
    others = [moved(place, dim, step) for dim in "xyz" for step in (1, -1)] + [moved(place, "core", 1)]
    for other in others:
        pl.semaphore_signal(barrier, inc=1, device_id=other, device_id_type=MESH)
    pl.semaphore_wait(barrier, len(others))


class Gather:
    def __init__(self, place, w, send, recv, block, order):
        self.place, self.w, self.send, self.recv = place, w, send, recv
        self.block, self.order = block, order

    def region(self, phase, value, half=None, core=None):
        index = {}
        for position, dim in enumerate(self.order):
            if position < phase:
                index.update(pick(dim, None))
            elif position == phase:
                index.update(pick(dim, value))
            else:
                index.update(pick(dim, self.place[dim]))
        rows = slice(None) if half is None else pl.ds(16 * half, 16)
        core = self.place["core"] if core is None else core
        return self.w.at[self.block, index["yl"], core, index["z"], index["yh"], index["x"], rows, :]

    def copy(self, k, ref, other):
        return pltpu.make_async_remote_copy(
            src_ref=ref,
            dst_ref=ref,
            send_sem=self.send.at[self.block, k],
            recv_sem=self.recv.at[self.block, k],
            device_id=other,
            device_id_type=MESH,
        )

    def ring(self, phase, k):
        dim = self.order[phase]
        me = self.place[dim]
        ahead, behind = moved(self.place, dim, 1), moved(self.place, dim, -1)
        if k == 0:
            return self.copy(4 * phase, self.region(phase, me), ahead)
        if k == 1:
            return self.copy(4 * phase + 1, self.region(phase, me), behind)
        if k == 2:
            return self.copy(4 * phase + 2, self.region(phase, (me + 3) % 4, 0), ahead)
        return self.copy(4 * phase + 3, self.region(phase, (me + 1) % 4, 1), behind)

    def arrival(self, phase, k):
        dim = self.order[phase]
        me = self.place[dim]
        other = moved(self.place, dim, -1 if k % 2 == 0 else 1)
        ref = (
            self.region(phase, (me + 3) % 4),
            self.region(phase, (me + 1) % 4),
            self.region(phase, (me + 2) % 4, 0),
            self.region(phase, (me + 2) % 4, 1),
        )[k]
        return self.copy(4 * phase + k, ref, other)

    def across(self, core):
        ref = self.w.at[self.block, :, core]
        return self.copy(12, ref, moved(self.place, "core", 1))

    def step(self, s):
        phase, part = divmod(s, 2)
        if part == 0:
            if phase > 0:
                self.arrival(phase - 1, 2).wait_recv()
                self.arrival(phase - 1, 3).wait_recv()
            if phase < 3:
                self.ring(phase, 0).start()
                self.ring(phase, 1).start()
            else:
                self.across(self.place["core"]).start()
        elif phase < 3:
            self.arrival(phase, 0).wait_recv()
            self.ring(phase, 2).start()
            self.arrival(phase, 1).wait_recv()
            self.ring(phase, 3).start()
        else:
            self.across(1 - self.place["core"]).wait_recv()

    def drain(self):
        for phase in range(3):
            for k in range(4):
                self.ring(phase, k).wait_send()
        self.across(self.place["core"]).wait_send()


GATHER_STEPS = 8


def gather_kernel(shard, w, send, recv, own):
    place = my_place()
    lat_y = place["y"]
    copy = pltpu.make_async_copy(
        shard, w.at[:, lat_y % 2, place["core"], place["z"], lat_y // 2, place["x"]], own
    )
    copy.start()
    greet(place)
    copy.wait()
    parts = [Gather(place, w, send, recv, b, ORDERS[b % 3]) for b in range(8)]
    for s in range(GATHER_STEPS):
        for part in parts:
            part.step(s)
    for part in parts:
        part.drain()


def gather(shard):
    return pl.pallas_call(
        gather_kernel,
        out_shape=jax.ShapeDtypeStruct((8, 2, 2, 4, 2, 4, 32, 256), BF16),
        in_specs=[pl.BlockSpec(memory_space=pl.ANY)],
        out_specs=pl.BlockSpec(memory_space=pl.ANY),
        scratch_shapes=[
            pltpu.SemaphoreType.DMA((8, 13)),
            pltpu.SemaphoreType.DMA((8, 13)),
            pltpu.SemaphoreType.DMA,
        ],
        compiler_params=pltpu.CompilerParams(collective_id=0, has_side_effects=True),
    )(shard)


def landing_shape(order, phase, columns):
    sizes = {"z": 4, "yh": 2, "x": 4, "yl": 2}
    for dim in order[: phase + 1]:
        for name in ("yh", "yl") if dim == "y" else (dim,):
            sizes[name] = 1
    return (sizes["z"], sizes["yh"], sizes["x"], sizes["yl"], 16, columns)


class Reduce:
    def __init__(self, place, p, landing, send, recv, order):
        self.place, self.p, self.landing = place, p, landing
        self.send, self.recv, self.order = send, recv, order

    def region(self, phase, value, part):
        index = {}
        for position, dim in enumerate(self.order):
            if position < phase:
                index.update(pick(dim, self.place[dim]))
            elif position == phase:
                index.update(pick(dim, value))
            else:
                index.update(pick(dim, None))
        columns = {None: slice(None), 0: pl.ds(0, 256), 1: pl.ds(256, self.p.shape[-1] - 256)}[part]
        return (self.place["core"], index["z"], index["yh"], index["x"], index["yl"], slice(None), columns)

    def copy(self, k, src, dst, other):
        return pltpu.make_async_remote_copy(
            src_ref=src,
            dst_ref=dst,
            send_sem=self.send.at[k],
            recv_sem=self.recv.at[k],
            device_id=other,
            device_id_type=MESH,
        )

    def across(self):
        return self.copy(12, self.p.at[1 - self.place["core"]], self.landing[12], moved(self.place, "core", 1))

    def ring(self, phase, k):
        dim = self.order[phase]
        me = self.place[dim]
        target = ((me + 2) % 4, (me + 2) % 4, (me + 1) % 4, (me + 3) % 4)[k]
        part = (0, 1, None, None)[k]
        other = moved(self.place, dim, 1 if k % 2 == 0 else -1)
        return self.copy(4 * phase + k, self.p.at[self.region(phase, target, part)], self.landing[4 * phase + k], other)

    def add(self, region, *landed):
        total = self.p[region].astype(F32)
        for ref in landed:
            total = total + ref[...].astype(F32)
        self.p[region] = total.astype(BF16)

    def step(self, s):
        if s == 0:
            self.across().start()
            return
        phase, part = divmod(s - 1, 2)
        land = self.landing
        if part == 0:
            if phase == 0:
                self.across().wait_recv()
                core = self.place["core"]
                for z in range(4):
                    self.p[core, z] = (self.p[core, z].astype(F32) + land[12][z].astype(F32)).astype(BF16)
            else:
                self.ring(phase - 1, 2).wait_recv()
                self.ring(phase - 1, 3).wait_recv()
                me = self.place[self.order[phase - 1]]
                self.add(self.region(phase - 1, me, None), land[4 * phase - 2], land[4 * phase - 1])
            if phase < 3:
                self.ring(phase, 0).start()
                self.ring(phase, 1).start()
        else:
            me = self.place[self.order[phase]]
            self.ring(phase, 0).wait_recv()
            self.add(self.region(phase, (me + 1) % 4, 0), land[4 * phase])
            self.ring(phase, 2).start()
            self.ring(phase, 1).wait_recv()
            self.add(self.region(phase, (me + 3) % 4, 1), land[4 * phase + 1])
            self.ring(phase, 3).start()

    def drain(self):
        for phase in range(3):
            for k in range(4):
                self.ring(phase, k).wait_send()
        self.across().wait_send()

    def result(self):
        y = self.place["y"]
        return self.p[self.place["core"], self.place["z"], y // 2, self.place["x"], y % 2].astype(F32)


REDUCE_STEPS = 8


def landing_shapes(order, columns):
    shapes = []
    for phase in range(3):
        for part in (256, columns - 256, columns, columns):
            shapes.append(pltpu.VMEM(landing_shape(order, phase, part), BF16))
    shapes.append(pltpu.VMEM((4, 2, 4, 2, 16, columns), BF16))
    return shapes


def unpacked(rows):
    return jnp.concatenate([rows[:8, :PACK], rows[8:, :PACK]], axis=1)


def spread_queries(lq):
    row = lax.broadcasted_iota(jnp.int32, (128, D), 0)
    head = lax.broadcasted_iota(jnp.int32, (128, D), 1) // 64
    total = jnp.zeros((128, D), F32)
    for q in range(LATENT):
        total = total + jnp.where(row == q * HEADS + head, lq[q : q + 1, :].astype(F32), 0.0)
    return total.astype(BF16)


def finish_gradients(factor, value_rows, out_rows, lq, grad_key, grad_value, grad_out):
    grad_value[...] = unpacked(value_rows) * factor
    grad_out[...] = unpacked(out_rows) * factor
    small = value_rows[:8, PACK:] * (factor * 0.125)
    high = small.astype(BF16)
    low = (small - high.astype(F32)).astype(BF16)
    queries = spread_queries(lq)
    grad_key[...] = dot(high, queries) + dot(low, queries)


def reduce_kernel(factor, pv_in, po_in, lq, grad_key, grad_value, grad_out, pv, po, send, recv, own, *landing):
    place = my_place()
    copies = [
        pltpu.make_async_copy(pv_in, pv, own.at[0]),
        pltpu.make_async_copy(po_in, po, own.at[1]),
    ]
    for copy in copies:
        copy.start()
    greet(place)
    for copy in copies:
        copy.wait()
    parts = [
        Reduce(place, pv, landing[:13], send.at[0], recv.at[0], ORDERS[0]),
        Reduce(place, po, landing[13:], send.at[1], recv.at[1], ORDERS[1]),
    ]
    for s in range(REDUCE_STEPS):
        for part in parts:
            part.step(s)
    for part in parts:
        part.drain()
    finish_gradients(factor, parts[0].result(), parts[1].result(), lq, grad_key, grad_value, grad_out)


def reduce_gradients(factor, pv, po, lq):
    vmem = pl.BlockSpec(memory_space=pltpu.VMEM)
    anywhere = pl.BlockSpec(memory_space=pl.ANY)
    return pl.pallas_call(
        functools.partial(reduce_kernel, factor),
        out_shape=[jax.ShapeDtypeStruct((8, D), F32)] * 3,
        in_specs=[anywhere, anywhere, vmem],
        out_specs=[vmem] * 3,
        scratch_shapes=[
            pltpu.VMEM(pv.shape, BF16),
            pltpu.VMEM(po.shape, BF16),
            pltpu.SemaphoreType.DMA((2, 13)),
            pltpu.SemaphoreType.DMA((2, 13)),
            pltpu.SemaphoreType.DMA((2,)),
        ]
        + landing_shapes(ORDERS[0], pv.shape[-1])
        + landing_shapes(ORDERS[1], po.shape[-1]),
        compiler_params=pltpu.CompilerParams(
            collective_id=1, has_side_effects=True, vmem_limit_bytes=48 * MIB
        ),
    )(pv, po, lq)


def resample_project(tok, kw, vw, lq, spread, values, logits):
    row = lax.broadcasted_iota(jnp.int32, (128, 768), 0)
    column = lax.broadcasted_iota(jnp.int32, (128, 768), 1)
    for cb in range(4):
        hit = row == (column // 256) * HEADS + cb * 4 + (column % 256) // 64
        spread[cb] = jnp.where(hit, 1.0, 0.0).astype(BF16)
    kq = dot(kw[...], spread_queries(lq), ((1,), (1,))) * 0.125
    high = kq.astype(BF16)
    low = (kq - high.astype(F32)).astype(BF16)

    def project(pair, _):
        rows = tok[pl.ds(pair * 2, 2)].reshape(416, D)
        for nb in range(4):
            part = dot(rows, vw[:, nb * 256 : (nb + 1) * 256]).astype(BF16)
            values[pl.ds(pair * 2, 2), :, nb * 256 : (nb + 1) * 256] = part.reshape(2, 208, 256)
        logits[pl.ds(pair * 2, 2)] = (dot(rows, high) + dot(rows, low)).reshape(2, 208, 128)
        return 0

    lax.fori_loop(0, GROUPS // 2, project, 0)


def resample_softmax(logits, weights):
    def group(g, _):
        x = logits[g].reshape(LEV, 16, 128)
        x = jnp.exp(x - jnp.max(x, axis=0, keepdims=True))
        x = x / jnp.sum(x, axis=0, keepdims=True)
        logits[g] = x.reshape(208, 128)
        weights[g] = x.astype(BF16).reshape(208, 128)
        return 0

    lax.fori_loop(0, GROUPS, group, 0)


def times_transposed(rows, ro, out):
    for nb in range(4):
        part = dot(rows[...].reshape(384, D), ro[nb * 256 : (nb + 1) * 256, :], ((1,), (1,)))
        out[:, :, nb * 256 : (nb + 1) * 256] = part.astype(BF16).reshape(GROUPS, 48, 256)


def resample_mix(values, weights, probs, spread, d_attended, attended, d_values, d_logits):
    def group(g, _):
        w = weights[g]
        d_weights = jnp.zeros((208, 128), F32)
        for cb in range(4):
            columns = slice(cb * 256, (cb + 1) * 256)
            wide = dot(w, spread[cb])
            v = values[g, :, columns].astype(F32).reshape(LEV, 16, 256)
            d_v = jnp.zeros((LEV, 16, 256), F32)
            products = []
            for q in range(LATENT):
                wq = wide[:, q * 256 : (q + 1) * 256].reshape(LEV, 16, 256)
                da = d_attended[g, q * 16 : (q + 1) * 16, columns].astype(F32)[None]
                attended[g, q * 16 : (q + 1) * 16, columns] = jnp.sum(wq * v, axis=0).astype(BF16)
                d_v = d_v + wq * da
                products.append((v * da).astype(BF16).reshape(208, 256))
            d_values[g, :, columns] = d_v.astype(BF16).reshape(208, 256)
            d_weights = d_weights + dot(jnp.concatenate(products, axis=1), spread[cb], ((1,), (1,)))
        p = probs[g].reshape(LEV, 16, 128)
        dw = d_weights.reshape(LEV, 16, 128)
        d_logits[g] = (p * (dw - jnp.sum(p * dw, axis=0, keepdims=True))).astype(BF16).reshape(208, 128)
        return 0

    lax.fori_loop(0, GROUPS, group, 0)


def resample_latents(attended, ro, lq, latents):
    rows = attended[...].reshape(384, D)
    for nb in range(4):
        columns = slice(nb * 256, (nb + 1) * 256)
        part = dot(rows, ro[:, columns]).reshape(GROUPS, LATENT, 16, 256)
        part = part + lq[:, columns].astype(F32)[None, :, None, :]
        latents[:, :, columns] = part.astype(BF16).reshape(GROUPS, 48, 256)


def pack_pair(left, right, p, z, columns):
    left = left.reshape(2, 4, 2, 2, 8, left.shape[-1])
    right = right.reshape(2, 4, 2, 2, 8, right.shape[-1])
    for core in range(2):
        both = jnp.concatenate([left[:, :, :, core], right[:, :, :, core]], axis=3)
        p[core, z, :, :, :, :, columns] = both.astype(BF16)


def resample_gradients(tok, grad, attended, d_values, d_logits, turned, pv, po):
    def block(z, _):
        columns = pl.ds(pl.multiple_of(z * 256, 256), 256)
        turned[...] = tok[:, :, columns].reshape(GROUPS * 208, 256).T
        for nb in range(2):
            halves = []
            for half in range(2):
                c = slice(half * PACK + nb * 256, half * PACK + (nb + 1) * 256)
                halves.append(dot(turned[...], d_values[:, :, c].reshape(GROUPS * 208, 256)))
            pack_pair(halves[0], halves[1], pv, z, slice(nb * 256, (nb + 1) * 256))
        small = dot(turned[...], d_logits[...].reshape(GROUPS * 208, 128))
        pack_pair(small, jnp.zeros_like(small), pv, z, slice(PACK, PACK + 128))
        turned[:, :384] = attended[:, :, columns].reshape(384, 256).T
        for nb in range(2):
            halves = []
            for half in range(2):
                c = slice(half * PACK + nb * 256, half * PACK + (nb + 1) * 256)
                halves.append(dot(turned[:, :384], grad[:, :, c].reshape(384, 256)))
            pack_pair(halves[0], halves[1], po, z, slice(nb * 256, (nb + 1) * 256))
        return 0

    lax.fori_loop(0, 4, block, 0)


RESAMPLE_SCRATCH = [
    pltpu.VMEM((4, 128, 768), BF16),
    pltpu.VMEM((GROUPS, 208, D), BF16),
    pltpu.VMEM((GROUPS, 208, 128), F32),
    pltpu.VMEM((GROUPS, 208, 128), BF16),
    pltpu.VMEM((GROUPS, 48, D), BF16),
    pltpu.VMEM((GROUPS, 48, D), BF16),
    pltpu.VMEM((GROUPS, 208, D), BF16),
    pltpu.VMEM((GROUPS, 208, 128), BF16),
    pltpu.VMEM((256, GROUPS * 208), BF16),
]


def resample_kernel(tok, grad, kw, vw, ro, lq, latents, pv, po, *scratch):
    spread, values, logits, weights, d_attended, attended, d_values, d_logits, turned = scratch
    resample_project(tok, kw, vw, lq, spread, values, logits)
    resample_softmax(logits, weights)
    times_transposed(grad, ro, d_attended)
    resample_mix(values, weights, logits, spread, d_attended, attended, d_values, d_logits)
    resample_latents(attended, ro, lq, latents)
    resample_gradients(tok, grad, attended, d_values, d_logits, turned, pv, po)


def resample(tok, grad, kw, vw, ro, lq):
    vmem = pl.BlockSpec(memory_space=pltpu.VMEM)
    return pl.pallas_call(
        resample_kernel,
        out_shape=[
            jax.ShapeDtypeStruct((GROUPS, 48, D), BF16),
            jax.ShapeDtypeStruct((2, 4, 2, 4, 2, 16, PACK + 128), BF16),
            jax.ShapeDtypeStruct((2, 4, 2, 4, 2, 16, PACK), BF16),
        ],
        in_specs=[vmem] * 6,
        out_specs=[vmem] * 3,
        scratch_shapes=RESAMPLE_SCRATCH,
        compiler_params=pltpu.CompilerParams(vmem_limit_bytes=56 * MIB),
    )(tok, grad, kw, vw, ro, lq)


def normalise(x, gain, normed):
    def window(w, _):
        rows = pl.ds(pl.multiple_of(w * 96, 96), 96)
        values = x[rows, :].astype(F32)
        centred = values - jnp.mean(values, axis=-1, keepdims=True)
        spread = jnp.mean(centred * centred, axis=-1, keepdims=True)
        normed[rows, :] = (centred * lax.rsqrt(spread + 1e-05) * gain).astype(BF16)
        return 0

    lax.fori_loop(0, 4, window, 0)


def attend_heads(j, layer, w, normed, bias, mixed):
    def part(block):
        return dot(normed[...], w[layer * 4 + block, j // 2, j % 2].reshape(D, 256))

    queries, keys, values = (part(0) * 0.125).astype(BF16), part(1).astype(BF16), part(2).astype(BF16)
    head = lax.broadcasted_iota(jnp.int32, (96, 256), 1) // 64
    columns = pl.ds(pl.multiple_of(j * 256, 256), 256)
    for win in range(4):
        rows = slice(win * 96, (win + 1) * 96)
        q, k, v = queries[rows], keys[rows], values[rows]
        stacked = jnp.concatenate([jnp.where(head == h, q, jnp.zeros_like(q)) for h in range(4)], axis=0)
        logits = dot(stacked, k, ((1,), (1,)))
        if bias is not None:
            logits = (logits.reshape(4, 96, 96) + bias[win][None]).reshape(384, 96)
        e = jnp.exp(logits - jnp.max(logits, axis=-1, keepdims=True))
        out = dot(e.astype(BF16), v) * (1.0 / jnp.sum(e, axis=-1, keepdims=True))
        total = jnp.zeros((96, 256), F32)
        for h in range(4):
            total = total + jnp.where(head == h, out[h * 96 : (h + 1) * 96], 0.0)
        mixed[rows, columns] = total.astype(BF16)


def sublayer_kernel(masked, *refs):
    if masked:
        x, gain, w, bias, out, normed, mixed = refs
    else:
        x, gain, w, out, normed, mixed = refs
        bias = None
    normalise(x, gain[...], normed)

    def heads(j, _):
        attend_heads(j, 0, w, normed, bias, mixed)
        return 0

    lax.fori_loop(0, 4, heads, 0)
    for j in range(4):
        columns = slice(j * 256, (j + 1) * 256)
        update = dot(mixed[...], w[3, j // 2, j % 2].reshape(D, 256))
        out[:, columns] = (x[:, columns].astype(F32) + update).astype(BF16)


def sublayer(x, gain, w, layer, bias):
    vmem = pl.BlockSpec(memory_space=pltpu.VMEM)
    extra = [] if bias is None else [bias]
    return pl.pallas_call(
        functools.partial(sublayer_kernel, bias is not None),
        grid=(1,),
        out_shape=jax.ShapeDtypeStruct((384, D), BF16),
        in_specs=[vmem, vmem, pl.BlockSpec((4,) + w.shape[1:], lambda i: (layer,) + (0,) * 7)] + [vmem] * len(extra),
        out_specs=vmem,
        scratch_shapes=[pltpu.VMEM((384, D), BF16), pltpu.VMEM((384, D), BF16)],
        compiler_params=pltpu.CompilerParams(vmem_limit_bytes=56 * MIB),
    )(x, gain, w, *extra)


def from_behind(block, axis, distance):
    count = lax.axis_size(axis)
    return lax.ppermute(block, axis, [((i - distance) % count, i) for i in range(count)])


def local(
    level_tokens,
    latent_query,
    key_weight,
    value_weight,
    resample_out,
    norm_gain,
    qkv_weight,
    out_weight,
    window_label,
    grad_latents,
):
    tok = level_tokens.reshape(2, GROUPS, 2, 4, LEV, D).transpose(1, 4, 2, 0, 3, 5).reshape(GROUPS, 208, D)
    grad = grad_latents.reshape(2, GROUPS, 2, 4, LATENT, D).transpose(1, 4, 2, 0, 3, 5).reshape(GROUPS, 48, D)
    shard = jnp.concatenate([qkv_weight.transpose(0, 2, 1, 3), out_weight[:, None]], axis=1).reshape(8, 32, 256)
    w = gather(shard)
    latents, pv, po = resample(tok, grad, key_weight, value_weight, resample_out, latent_query)
    factor = (2 * 64 * lax.axis_size("lat") * lax.axis_size("lon")) ** (-0.5)
    grad_key, grad_value, grad_out = reduce_gradients(factor, pv, po, latent_query)

    tiles = lax.all_to_all(latents.reshape(4, 2, 48, D), "lon", split_axis=0, concat_axis=0, tiled=True)
    x = tiles.reshape(2, 2, 2, 48, D).swapaxes(1, 2).reshape(384, D)
    middle = sublayer(x, norm_gain[0:1], w, 0, None)
    cells = middle.reshape(2, 2, 2, LATENT, 2, 8, D).transpose(0, 2, 1, 4, 3, 5, 6).reshape(4, 4, LATENT, 8, D)
    cells = jnp.concatenate([cells[1:], from_behind(cells[:1], "lat", -1)], axis=0)
    cells = jnp.concatenate([cells[:, 1:], from_behind(cells[:, :1], "lon", -1)], axis=1)
    rolled = cells.reshape(2, 2, 2, 2, LATENT, 8, D).transpose(0, 2, 1, 4, 3, 5, 6).reshape(384, D)

    row = lax.axis_index("lat") * 8 + jnp.arange(8, dtype=jnp.int32)
    codes = window_label * 2 + (row >= 8 * lax.axis_size("lat") - 2).astype(jnp.int32)[:, None]
    codes = codes.reshape(2, 2, 2, 2, 2, 4).transpose(0, 3, 1, 4, 2, 5)
    codes = jnp.broadcast_to(codes[:, :, :, None], (2, 2, 2, LATENT, 2, 2, 4)).reshape(4, 96)
    bias = jnp.where(codes[:, :, None] == codes[:, None, :], 0.0, -1e30).astype(F32)
    out = sublayer(rolled, norm_gain[1:2], w, 1, bias)
    out = out.reshape(2, 2, 2, LATENT, 2, 2, 4, D).transpose(0, 2, 5, 1, 4, 6, 3, 7).reshape(8, 16, LATENT, D)
    return (out, grad_key, grad_value, grad_out)


def solution(mesh):
    in_specs = (
        P(("lat", "lon"), None, None, None),
        P(),
        P(),
        P(),
        P(),
        P(),
        P(None, "lat", None, "lon"),
        P(None, "lat", "lon"),
        P("lat", "lon"),
        P(("lat", "lon"), None, None, None),
    )
    out_specs = (
        P("lat", "lon", None, None),
        P(("lat", "lon"), None),
        P(("lat", "lon"), None),
        P(("lat", "lon"), None),
    )
    return jax.shard_map(local, mesh=mesh, in_specs=in_specs, out_specs=out_specs, check_vma=False)
```

time: 2100 us -> 204 us (0.10)
  waiting for transfers between devices: 1740 us -> 4.33 us
  Pallas kernels: 0 us -> 154 us
  local copies, waits for them, and re-layouts: 178 us -> 28.1 us
  matrix products: 102 us -> 0 us
  blocking collectives: 25 us -> 0 us
    unnamed x9 -> x0, waiting for transfers between devices: 1090 us -> none
    reduce_scatter x1 -> x0, waiting for transfers between devices: 641 us -> none  [local(): lax.psum_scatter(grad_out * factor, ('lat', 'lon'), scatter_dimension=0,...]
    pallas_call x0 -> x5, Pallas kernels: none -> 154 us  [the longest x1 64 us: gather(): pl.pallas_call(gather_kernel, out_shape=jax.ShapeDtypeStruct((8, 2, 2, 4,...]
    dot_general x20 -> x0, matrix products: 102 us -> none  [the longest x2 16.9 us: sublayer(): jnp.dot(tile_flat, weight_piece.reshape(weight_piece.shape[0], -1), prefe...]
    reshape x11 -> x10, local copies, waits for them, and re-layouts: 63.4 us -> 20.8 us  [the longest x3 9.33 us: local(): level_tokens.reshape(2, GROUPS, 2, 4, LEV, D).transpose(1, 4, 2, 0, 3, 5)]
    unnamed x34 -> x19, local copies, waits for them, and re-layouts: 37.8 us -> 3.46 us
    convert_element_type x7 -> x0, local copies, waits for them, and re-layouts: 32 us -> none  [the longest x1 11.4 us: resample(): d_keys = d_keys.astype(jnp.bfloat16).reshape(-1, model_width)]
    all_gather x4 -> x0, blocking collectives: 25 us -> none  [the longest x2 13.4 us: sublayer(): wide_weight = lax.all_gather(weight_shard, 'lon', axis=2, tiled=True)]
  transfers between devices with their start and end apart: 10 -> 3, of which waited for: 5 -> 1; matrix products, arithmetic and copies ran while one was open for 14% -> 2% of each run, Pallas kernels for 0% -> 50%
where the time goes in v1:
time: 204 us; the launch traced here: 201 us
  Pallas kernels  154 us (75%)
  local copies, waits for them, and re-layouts  28.1 us (14%)
  starting transfers between devices  9.84 us (5%)
  waiting for transfers between devices  4.33 us (2%)
  other arithmetic  3.4 us (2%)
    pallas_call x1, Pallas kernels, gather(): pl.pallas_call(gather_kernel, out_shape=jax.ShapeDtypeStruct((8, 2, 2, 4,...  64 us
    pallas_call x1, Pallas kernels, reduce_gradients(): pl.pallas_call(functools.partial(reduce_kernel, factor), out_shape=[jax.S...  35.5 us
    pallas_call x1, Pallas kernels, resample(): pl.pallas_call(resample_kernel, out_shape=[jax.ShapeDtypeStruct((GROUPS,...  28.7 us
    pallas_call x2, Pallas kernels, sublayer(): pl.pallas_call(functools.partial(sublayer_kernel, bias is not None), grid...  26.3 us
    reshape x3, local copies, waits for them, and re-layouts, local(): level_tokens.reshape(2, GROUPS, 2, 4, LEV, D).transpose(1, 4, 2, 0, 3, 5)  9.33 us
    reshape x3, local copies, waits for them, and re-layouts, local(): grad_latents.reshape(2, GROUPS, 2, 4, LATENT, D).transpose(1, 4, 2, 0, 3, 5)  7.27 us
    ppermute x2, starting transfers between devices, from_behind(): lax.ppermute(block, axis, [((i - distance) % count, i) for i in range(cou...  4.96 us
    all_to_all x1, starting transfers between devices, local(): lax.all_to_all(latents.reshape(4, 2, 48, D), 'lon', split_axis=0, concat_...  4.88 us
  transfers between devices with their start and end apart: 3, of which 1 were waited for; matrix products, arithmetic and copies ran while one was open for 2% of the time, Pallas kernels for 50%

profile of v1, /device:TPU:1, one launch (start us, length us, event | category | flops | bytes accessed | tf_op | source)
XLA Modules:
  0.0 200.9 jit_solution(1967780454001865378)
XLA Ops:
  0.6 2.5 %reshape.64 = bf16[2,8,2,4,3,1024]{5,3,2,1,4,0:T(4,128)(2,1)} reshape(bf16[2,64,3,1024]{3,1,2,0:T(8,128)(2,1)} %param.19) | data formatting | bytes 1572864 | tf_op jit(solution)/shard_map/reshape | solution.py:584
  3.2 2.5 %copy.30 = bf16[2,8,2,4,3,1024]{5,3,0,2,4,1:T(4,128)(2,1)} copy(bf16[2,8,2,4,3,1024]{5,3,2,1,4,0:T(4,128)(2,1)} %reshape.64) | data formatting | bytes 1572864 | tf_op jit(solution)/shard_map/reshape | solution.py:584
  5.7 2.3 %reshape.65.grad = bf16[8,48,1024]{2,1,0:T(8,128)(2,1)} reshape(bf16[8,3,2,2,4,1024]{5,4,3,2,1,0:T(4,128)(2,1)} %bitcast.44) | data formatting | bytes 1572864 | tf_op jit(solution)/shard_map/reshape | solution.py:584
  7.9 2.8 %reshape.62 = bf16[2,8,2,4,13,1024]{5,3,2,1,4,0:T(4,128)(2,1)} reshape(bf16[2,64,13,1024]{3,1,2,0:T(8,128)(2,1)S(1)} %copy-done.3) | data formatting | bytes 6815744 | tf_op jit(solution)/shard_map/reshape | solution.py:583
  10.7 4.0 %copy.29 = bf16[2,8,2,4,13,1024]{5,3,0,2,4,1:T(4,128)(2,1)S(1)} copy(bf16[2,8,2,4,13,1024]{5,3,2,1,4,0:T(4,128)(2,1)} %reshape.62) | data formatting | bytes 6815744 | tf_op jit(solution)/shard_map/reshape | solution.py:583
  14.7 2.5 %reshape.63.tok = bf16[8,208,1024]{2,1,0:T(8,128)(2,1)} reshape(bf16[8,13,2,2,4,1024]{5,4,3,2,1,0:T(4,128)(2,1)S(1)} %bitcast.36) | data formatting | bytes 6815744 | tf_op jit(solution)/shard_map/reshape | solution.py:583
  17.3 28.7 %shard_map.129 = (bf16[8,48,1024]{2,1,0:T(8,128)(2,1)}, bf16[2,4,2,4,2,16,640]{6,5,4,3,2,1,0:T(8,128)(2,1)}, bf16[2,4,2,4,2,16,512]{6,5,4,3,2,1,0:T(8,128)(2,1)}) custom-call(bf16[8,208,1024]{2,1,0:T(8,128)(2,1)} %reshape.63.tok, bf16[8,48,1024]{2,1,0:T(8,128)(2,1)} %reshape.65.grad, bf16[1024,1024]{1,0:T(8,128)(2,1)} %kw.1, bf16[1024,1024]{1,0:T(8,128)(2,1)} %vw.1, ...), custom_call_target="tpu_custom_call" | custom-call | tf_op jit(solution)/shard_map/pallas_call | solution.py:485
  46.0 4.9 %all-to-all-start = ((bf16[4,2,48,1024]{3,2,1,0:T(8,128)(2,1)}), bf16[4,2,48,1024]{3,2,1,0:T(8,128)(2,1)S(1)}, u32[]{:S(2)}, u32[]{:S(2)}) async-start(bf16[4,2,48,1024]{3,2,1,0:T(8,128)(2,1)} %bitcast.46), calls=%async_computation | async-start | bytes 1572864 | tf_op jit(solution)/shard_map/all_to_all | solution.py:591
  50.9 0.7 pad_maximum_fusion.2
  51.5 64.0 %shard_map.130.refs_2_ = bf16[8,2,2,4,2,4,32,256]{7,6,5,4,3,2,1,0:T(8,128)(2,1)} custom-call(bf16[8,32,256]{2,1,0:T(8,128)(2,1)} %bitcast.47), custom_call_target="tpu_custom_call" | custom-call | tf_op jit(solution)/shard_map/pallas_call | solution.py:167
  115.6 0.6 fusion.1
  116.2 1.0 copy.21
  117.1 13.1 %shard_map.131 = bf16[384,1024]{1,0:T(8,128)(2,1)} custom-call(bf16[384,1024]{1,0:T(8,128)(2,1)} %bitcast.38, f32[1,1024]{1,0:T(1,128)} %get-tuple-element.17.refs_1_, bf16[8,2,2,4,2,4,32,256]{7,6,5,4,3,2,1,0:T(8,128)(2,1)} %shard_map.130.refs_2_), custom_call_target="tpu_custom_call" | custom-call | tf_op jit(solution)/shard_map/pallas_call | solution.py:555
  130.3 1.3 copy.23
  131.6 0.7 slice.25
  132.3 4.2 %collective-permute-start = (bf16[1,4,3,8,1024]{4,3,2,1,0:T(8,128)(2,1)}, bf16[1,4,3,8,1024]{4,3,2,1,0:T(8,128)(2,1)}, u32[]{:S(2)}, u32[]{:S(2)}) collective-permute-start(bf16[1,4,3,8,1024]{4,3,2,1,0:T(8,128)(2,1)} %slice.25), channel_id=1, source_target_pairs={{4,0},{8,4},{12,8},{16,12},{20,16},{24,20},{28,24},{32,28},{36,32}... | collective-permute-start | bytes 589832 | tf_op jit(solution)/shard_map/ppermute | solution.py:568
  136.7 0.1 eq.15
  136.8 4.3 %collective-permute-done = bf16[1,4,3,8,1024]{4,3,2,1,0:T(8,128)(2,1)} collective-permute-done((bf16[1,4,3,8,1024]{4,3,2,1,0:T(8,128)(2,1)}, bf16[1,4,3,8,1024]{4,3,2,1,0:T(8,128)(2,1)}, u32[]{:S(2)}, u32[]{:S(2)}) %collective-permute-start) | collective-permute-done | bytes 196640 | tf_op jit(solution)/shard_map/ppermute | solution.py:568
  141.2 0.8 pad_maximum_fusion.1
  142.0 0.8 collective-permute-start.1
  142.8 0.8 compare_select_fusion.refs_3_
  143.6 1.6 copy-done.1
  145.2 35.5 %shard_map.133 = (f32[8,1024]{1,0:T(8,128)S(1)}, f32[8,1024]{1,0:T(8,128)S(1)}, f32[8,1024]{1,0:T(8,128)S(1)}) custom-call(bf16[2,4,2,4,2,16,640]{6,5,4,3,2,1,0:T(8,128)(2,1)S(1)} %copy-done, bf16[2,4,2,4,2,16,512]{6,5,4,3,2,1,0:T(8,128)(2,1)S(1)} %copy-done.1, bf16[3,1024]{1,0:T(4,128)(2,1)S(1)} %copy-done.2), custom_call_target="tpu_custom_call" | custom-call | tf_op jit(solution)/shard_map/pallas_call | solution.py:334
  180.7 1.0 fusion
  181.8 0.9 copy.24
  182.7 13.1 %shard_map.132 = bf16[384,1024]{1,0:T(8,128)(2,1)} custom-call(bf16[384,1024]{1,0:T(8,128)(2,1)} %bitcast.37, f32[1,1024]{1,0:T(1,128)} %get-tuple-element.16.refs_1_, bf16[8,2,2,4,2,4,32,256]{7,6,5,4,3,2,1,0:T(8,128)(2,1)} %shard_map.130.refs_2_, f32[4,96,96]{2,1,0:T(8,128)} %compare_select_fusion.refs_3_), custom_call_target="tpu_custom_call" | custom-call | tf_op jit(solution)/shard_map/pallas_call | solution.py:555
  195.8 1.7 reshape.75
  197.5 0.5 copy.26
  198.0 1.1 reshape.76
  199.1 0.6 copy.34
  199.7 0.6 copy.35
  200.3 0.6 copy.36
  (24 shorter events, 0.3 us)
Async XLA Ops:
  0.6 7.3 %copy-start.3 = (bf16[2,64,13,1024]{3,1,2,0:T(8,128)(2,1)S(1)}, bf16[2,64,13,1024]{3,1,2,0:T(8,128)(2,1)}, u32[]{:S(2)}) copy-start(bf16[2,64,13,1024]{3,1,2,0:T(8,128)(2,1)} %param.10) | copy-start | bytes 10223620
  17.3 33.6 %copy-start.4 = (bf16[2,32,3,256]{3,1,2,0:T(8,128)(2,1)S(1)}, bf16[2,32,3,256]{3,1,2,0:T(8,128)(2,1)}, u32[]{:S(2)}) copy-start(bf16[2,32,3,256]{3,1,2,0:T(8,128)(2,1)} %param.16) | copy-start | bytes 294916
  17.3 33.6 %copy-start.5 = (bf16[2,32,256]{2,1,0:T(8,128)(2,1)S(1)}, bf16[2,32,256]{2,1,0:T(8,128)(2,1)}, u32[]{:S(2)}) copy-start(bf16[2,32,256]{2,1,0:T(8,128)(2,1)} %param.17) | copy-start | bytes 98308
  46.0 70.2 %all-to-all-start = ((bf16[4,2,48,1024]{3,2,1,0:T(8,128)(2,1)}), bf16[4,2,48,1024]{3,2,1,0:T(8,128)(2,1)S(1)}, u32[]{:S(2)}, u32[]{:S(2)}) async-start(bf16[4,2,48,1024]{3,2,1,0:T(8,128)(2,1)} %bitcast.46), calls=%async_computation | async-start | bytes 1572864 | tf_op jit(solution)/shard_map/all_to_all | solution.py:591
  51.5 64.0 %copy-start.6 = (f32[2,1024]{1,0:T(2,128)S(1)}, f32[2,1024]{1,0:T(2,128)}, u32[]{:S(2)}) copy-start(f32[2,1024]{1,0:T(2,128)} %param.15) | copy-start | bytes 24580
  117.1 19.3 %copy-start.7 = (s32[8,16]{1,0:T(8,128)S(1)}, s32[8,16]{1,0:T(8,128)}, u32[]{:S(2)}) copy-start(s32[8,16]{1,0:T(8,128)} %param.18) | copy-start | bytes 1540
  130.3 13.3 %copy-start = (bf16[2,4,2,4,2,16,640]{6,5,4,3,2,1,0:T(8,128)(2,1)S(1)}, bf16[2,4,2,4,2,16,640]{6,5,4,3,2,1,0:T(8,128)(2,1)}, u32[]{:S(2)}) copy-start(bf16[2,4,2,4,2,16,640]{6,5,4,3,2,1,0:T(8,128)(2,1)} %get-tuple-element.11.pv_in) | copy-start | bytes 7864324
  130.3 13.3 %copy-start.2 = (bf16[3,1024]{1,0:T(4,128)(2,1)S(1)}, bf16[3,1024]{1,0:T(4,128)(2,1)}, u32[]{:S(2)}) copy-start(bf16[3,1024]{1,0:T(4,128)(2,1)} %lq.3) | copy-start | bytes 18436
  132.3 8.8 %collective-permute-start = (bf16[1,4,3,8,1024]{4,3,2,1,0:T(8,128)(2,1)}, bf16[1,4,3,8,1024]{4,3,2,1,0:T(8,128)(2,1)}, u32[]{:S(2)}, u32[]{:S(2)}) collective-permute-start(bf16[1,4,3,8,1024]{4,3,2,1,0:T(8,128)(2,1)} %slice.25), channel_id=1, source_target_pairs={{4,0},{8,4},{12,8},{16,12},{20,16},{24,20},{28,24},{32,28},{36,32}... | collective-permute-start | bytes 589832 | tf_op jit(solution)/shard_map/ppermute | solution.py:568
  142.0 39.7 %collective-permute-start.1 = (bf16[4,1,3,8,1024]{4,3,2,1,0:T(8,128)(2,1)S(1)}, bf16[4,1,3,8,1024]{4,3,2,1,0:T(8,128)(2,1)S(1)}, u32[]{:S(2)}, u32[]{:S(2)}) collective-permute-start(bf16[4,1,3,8,1024]{4,3,2,1,0:T(8,128)(2,1)S(1)} %pad_maximum_fusion.1), channel_id=1, source_target_pairs={{1,0},{2,1},{3,2},{0,3},{5,4},{6,5},{7,6},{4,7},{9,8},{10,9},{11,1... | collective-permute-start | bytes 589832 | tf_op jit(solution)/shard_map/ppermute | solution.py:568
  143.6 1.6 copy-start.1

commit v2 on v1

v2 whole, which is shorter than its diff:
```python
import functools

import jax
import jax.numpy as jnp
from jax import lax
from jax.experimental import pallas as pl
from jax.experimental.pallas import tpu as pltpu
from jax.sharding import PartitionSpec as P

MESH = pl.DeviceIdType.MESH
F32, BF16 = jnp.float32, jnp.bfloat16
D = 1024
HEADS = 16
LEV = 13
LATENT = 3
GROUPS = 8
MIB = 1024 * 1024


def dot(a, b, dims=((1,), (0,))):
    return lax.dot_general(a, b, (dims, ((), ())), preferred_element_type=F32)


def my_place():
    lat, lon = lax.axis_index("lat"), lax.axis_index("lon")
    return {
        "z": lat // 8,
        "y": ((lat // 4) % 2) * 2 + lon // 2,
        "x": lat % 4,
        "core": lon % 2,
    }


def device_of(place):
    lat = place["z"] * 8 + (place["y"] // 2) * 4 + place["x"]
    return (lat, (place["y"] % 2) * 2 + place["core"])


def moved(place, dim, delta):
    size = 2 if dim == "core" else 4
    other = dict(place)
    other[dim] = (place[dim] + delta + size) % size
    return device_of(other)


def pick(dim, value):
    if dim == "y":
        if value is None:
            return {"yh": slice(None), "yl": slice(None)}
        return {"yh": pl.ds(value // 2, 1), "yl": pl.ds(value % 2, 1)}
    return {dim: slice(None) if value is None else pl.ds(value, 1)}


def greet(place):
    barrier = pltpu.get_barrier_semaphore()
    others = [moved(place, dim, step) for dim in "xyz" for step in (1, -1)] + [moved(place, "core", 1)]
    lat, lon = device_of(place)
    others += [(lat, (lon + k) % 4) for k in range(1, 4)]
    others += [((lat + step) % 32, (lon + turn) % 4) for step, turn in ((1, 0), (31, 0), (1, 1), (31, 3))]
    for other in others:
        pl.semaphore_signal(barrier, inc=1, device_id=other, device_id_type=MESH)
    pl.semaphore_wait(barrier, len(others))


PARTS = (
    ((0, 3, ("x", "y", "z")), (3, 3, ("y", "z", "x")), (6, 2, ("z", "x", "y"))),
    ((8, 3, ("z", "x", "y")), (11, 3, ("x", "y", "z")), (14, 2, ("y", "z", "x"))),
)


class Gather:
    def __init__(self, place, w, send, recv, number, part):
        self.place, self.w, self.send, self.recv, self.number = place, w, send, recv, number
        first, count, self.order = part
        self.tiles = pl.ds(first, count)

    def region(self, phase, value, half=None):
        index = {}
        for position, dim in enumerate(self.order):
            if position < phase:
                index.update(pick(dim, None))
            elif position == phase:
                index.update(pick(dim, value))
            else:
                index.update(pick(dim, self.place[dim]))
        rows = slice(None) if half is None else pl.ds(16 * half, 16)
        core = self.place["core"]
        return self.w.at[self.tiles, index["yl"], core, index["z"], index["yh"], index["x"], rows, :]

    def copy(self, k, ref, other):
        return pltpu.make_async_remote_copy(
            src_ref=ref,
            dst_ref=ref,
            send_sem=self.send.at[self.number, k],
            recv_sem=self.recv.at[self.number, k],
            device_id=other,
            device_id_type=MESH,
        )

    def ring(self, phase, k):
        dim = self.order[phase]
        me = self.place[dim]
        other = moved(self.place, dim, 1 if k % 2 == 0 else -1)
        if k < 2:
            return self.copy(4 * phase + k, self.region(phase, me), other)
        return self.copy(4 * phase + k, self.region(phase, (me + 7 - 2 * k) % 4, k - 2), other)

    def arrival(self, phase, k):
        dim = self.order[phase]
        me = self.place[dim]
        other = moved(self.place, dim, -1 if k % 2 == 0 else 1)
        if k < 2:
            return self.copy(4 * phase + k, self.region(phase, (me + 3 + 2 * k) % 4), other)
        return self.copy(4 * phase + k, self.region(phase, (me + 2) % 4, k - 2), other)

    def across(self, core):
        return self.copy(12, self.w.at[self.tiles, :, core], moved(self.place, "core", 1))

    def step(self, s):
        phase, part = divmod(s, 2)
        if part == 0:
            if phase > 0:
                self.arrival(phase - 1, 2).wait_recv()
                self.arrival(phase - 1, 3).wait_recv()
            if phase < 3:
                self.ring(phase, 0).start()
                self.ring(phase, 1).start()
            else:
                self.across(self.place["core"]).start()
        elif phase < 3:
            self.arrival(phase, 0).wait_recv()
            self.ring(phase, 2).start()
            self.arrival(phase, 1).wait_recv()
            self.ring(phase, 3).start()
        else:
            self.across(1 - self.place["core"]).wait_recv()

    def drain(self):
        for phase in range(3):
            for k in range(4):
                self.ring(phase, k).wait_send()
        self.across(self.place["core"]).wait_send()


def landing_shape(order, phase, columns):
    sizes = {"z": 4, "yh": 2, "x": 4, "yl": 2}
    for dim in order[: phase + 1]:
        for name in ("yh", "yl") if dim == "y" else (dim,):
            sizes[name] = 1
    return (sizes["z"], sizes["yh"], sizes["x"], sizes["yl"], 16, columns)


HALF = {256: 128, 384: 128, 512: 256}


class Reduce:
    def __init__(self, place, p, landing, send, recv, order):
        self.place, self.p, self.landing = place, p, landing
        self.send, self.recv, self.order = send, recv, order

    def region(self, phase, value, part):
        index = {}
        for position, dim in enumerate(self.order):
            if position < phase:
                index.update(pick(dim, self.place[dim]))
            elif position == phase:
                index.update(pick(dim, value))
            else:
                index.update(pick(dim, None))
        width = self.p.shape[-1]
        cut = HALF[width]
        columns = {None: slice(None), 0: pl.ds(0, cut), 1: pl.ds(cut, width - cut)}[part]
        return (self.place["core"], index["z"], index["yh"], index["x"], index["yl"], slice(None), columns)

    def copy(self, k, src, dst, other):
        return pltpu.make_async_remote_copy(
            src_ref=src,
            dst_ref=dst,
            send_sem=self.send.at[k],
            recv_sem=self.recv.at[k],
            device_id=other,
            device_id_type=MESH,
        )

    def across(self):
        return self.copy(12, self.p.at[1 - self.place["core"]], self.landing[12], moved(self.place, "core", 1))

    def ring(self, phase, k):
        dim = self.order[phase]
        me = self.place[dim]
        target = ((me + 2) % 4, (me + 2) % 4, (me + 1) % 4, (me + 3) % 4)[k]
        part = (0, 1, None, None)[k]
        other = moved(self.place, dim, 1 if k % 2 == 0 else -1)
        return self.copy(4 * phase + k, self.p.at[self.region(phase, target, part)], self.landing[4 * phase + k], other)

    def add(self, region, *landed):
        total = self.p[region].astype(F32)
        for ref in landed:
            total = total + ref[...].astype(F32)
        self.p[region] = total.astype(BF16)

    def step(self, s):
        if s == 0:
            self.across().start()
            return
        phase, part = divmod(s - 1, 2)
        land = self.landing
        if part == 0:
            if phase == 0:
                self.across().wait_recv()
                core = self.place["core"]
                for z in range(4):
                    self.p[core, z] = (self.p[core, z].astype(F32) + land[12][z].astype(F32)).astype(BF16)
            else:
                self.ring(phase - 1, 2).wait_recv()
                self.ring(phase - 1, 3).wait_recv()
                me = self.place[self.order[phase - 1]]
                self.add(self.region(phase - 1, me, None), land[4 * phase - 2], land[4 * phase - 1])
            if phase < 3:
                self.ring(phase, 0).start()
                self.ring(phase, 1).start()
        else:
            me = self.place[self.order[phase]]
            self.ring(phase, 0).wait_recv()
            self.add(self.region(phase, (me + 1) % 4, 0), land[4 * phase])
            self.ring(phase, 2).start()
            self.ring(phase, 1).wait_recv()
            self.add(self.region(phase, (me + 3) % 4, 1), land[4 * phase + 1])
            self.ring(phase, 3).start()

    def drain(self):
        for phase in range(3):
            for k in range(4):
                self.ring(phase, k).wait_send()
        self.across().wait_send()

    def result(self):
        y = self.place["y"]
        return self.p[self.place["core"], self.place["z"], y // 2, self.place["x"], y % 2].astype(F32)


def landing_shapes(order, columns):
    shapes = []
    for phase in range(3):
        for part in (HALF[columns], columns - HALF[columns], columns, columns):
            shapes.append(pltpu.VMEM(landing_shape(order, phase, part), BF16))
    shapes.append(pltpu.VMEM((4, 2, 4, 2, 16, columns), BF16))
    return shapes


def spread_queries(lq):
    row = lax.broadcasted_iota(jnp.int32, (128, D), 0)
    head = lax.broadcasted_iota(jnp.int32, (128, D), 1) // 64
    total = jnp.zeros((128, D), F32)
    for q in range(LATENT):
        total = total + jnp.where(row == q * HEADS + head, lq[q : q + 1, :].astype(F32), 0.0)
    return total.astype(BF16)


def finish_gradients(factor, sums, lq, grad_key, grad_value, grad_out):
    first, second, third = sums
    grad_value[:, 0:256] = first[:8, :256] * factor
    grad_value[:, 256:512] = second[:8] * factor
    grad_value[:, 512:768] = first[8:, :256] * factor
    grad_value[:, 768:1024] = second[8:] * factor
    grad_out[:, 0:512] = third[:8] * factor
    grad_out[:, 512:1024] = third[8:] * factor
    small = first[:8, 256:] * (factor * 0.125)
    high = small.astype(BF16)
    low = (small - high.astype(F32)).astype(BF16)
    queries = spread_queries(lq)
    grad_key[...] = dot(high, queries) + dot(low, queries)


def looped(count, body, hooks):
    def step(i, _):
        body(i)
        for at, hook in hooks.items():
            pl.when(i == at)(hook)
        return 0

    lax.fori_loop(0, count, step, 0)


def group_at(g):
    return g // 4, pl.ds(pl.multiple_of((g % 4) * 16, 16), 16)


def spread_heads(spread):
    row = lax.broadcasted_iota(jnp.int32, (128, 768), 0)
    column = lax.broadcasted_iota(jnp.int32, (128, 768), 1)
    for cb in range(4):
        hit = row == (column // 256) * HEADS + cb * 4 + (column % 256) // 64
        spread[cb] = jnp.where(hit, 1.0, 0.0).astype(BF16)


def key_queries(kw, lq, kq):
    queries = spread_queries(lq)

    def rows(i, _):
        at = pl.ds(pl.multiple_of(i * 256, 256), 256)
        total = dot(kw[at, :], queries, ((1,), (1,))) * 0.125
        high = total.astype(BF16)
        kq[0, at, :] = high
        kq[1, at, :] = (total - high.astype(F32)).astype(BF16)
        return 0

    lax.fori_loop(0, 4, rows, 0)


def resample_project(tok, vw, kq, values, logits, hooks):
    def project(r):
        rows = tok[r].reshape(LEV * 64, D)
        for nb in range(4):
            columns = slice(nb * 256, (nb + 1) * 256)
            values[r, :, :, columns] = dot(rows, vw[:, columns]).astype(BF16).reshape(LEV, 64, 256)
        logits[r] = (dot(rows, kq[0]) + dot(rows, kq[1])).reshape(LEV, 64, 128)

    looped(2, project, hooks)


def resample_softmax(logits, weights):
    def group(g, _):
        r, c = group_at(g)
        x = logits[r, :, c]
        x = jnp.exp(x - jnp.max(x, axis=0, keepdims=True))
        x = x / jnp.sum(x, axis=0, keepdims=True)
        logits[r, :, c] = x
        weights[r, :, c] = x.astype(BF16)
        return 0

    lax.fori_loop(0, GROUPS, group, 0)


def resample_cotangents(grad, ro, d_attended):
    rows = grad[...].reshape(384, D)
    for nb in range(4):
        columns = slice(nb * 256, (nb + 1) * 256)
        part = dot(rows, ro[columns, :], ((1,), (1,)))
        d_attended[:, :, :, columns] = part.astype(BF16).reshape(2, LATENT, 64, 256)


def resample_mix(values, weights, probs, spread, d_attended, attended, d_logits, hooks):
    def group(g):
        r, c = group_at(g)
        w = weights[r, :, c].reshape(208, 128)
        d_weights = jnp.zeros((208, 128), F32)
        for cb in range(4):
            columns = slice(cb * 256, (cb + 1) * 256)
            wide = dot(w, spread[cb])
            v = values[r, :, c, columns].astype(F32)
            d_v = jnp.zeros((LEV, 16, 256), F32)
            products = []
            for q in range(LATENT):
                wq = wide[:, q * 256 : (q + 1) * 256].reshape(LEV, 16, 256)
                da = d_attended[r, q, c, columns].astype(F32)[None]
                attended[r, q, c, columns] = jnp.sum(wq * v, axis=0).astype(BF16)
                d_v = d_v + wq * da
                products.append((v * da).astype(BF16).reshape(208, 256))
            values[r, :, c, columns] = d_v.astype(BF16)
            d_weights = d_weights + dot(jnp.concatenate(products, axis=1), spread[cb], ((1,), (1,)))
        p = probs[r, :, c]
        dw = d_weights.reshape(LEV, 16, 128)
        d_logits[r, :, c] = (p * (dw - jnp.sum(p * dw, axis=0, keepdims=True))).astype(BF16)

    looped(GROUPS, group, hooks)


def resample_latents(attended, ro, lq, latents):
    rows = attended[...].reshape(384, D)
    for nb in range(4):
        columns = slice(nb * 256, (nb + 1) * 256)
        part = dot(rows, ro[:, columns]).reshape(2, LATENT, 64, 256)
        part = part + lq[:, columns].astype(F32)[None, :, None, :]
        latents[:, :, :, columns] = part.astype(BF16)


def pack_pair(left, right, p, z, columns):
    left = left.reshape(2, 4, 2, 2, 8, left.shape[-1])
    right = right.reshape(2, 4, 2, 2, 8, right.shape[-1])
    for core in range(2):
        both = jnp.concatenate([left[:, :, :, core], right[:, :, :, core]], axis=3)
        p[core, z, :, :, :, :, columns] = both.astype(BF16)


def resample_gradients(tok, grad, attended, d_values, d_logits, turned, packed, hooks):
    first, second, third = packed

    def block(z):
        columns = pl.ds(pl.multiple_of(z * 256, 256), 256)
        turned[...] = tok[:, :, :, columns].reshape(GROUPS * 208, 256).T
        for nb in range(2):
            halves = []
            for half in range(2):
                c = slice(half * 512 + nb * 256, half * 512 + (nb + 1) * 256)
                halves.append(dot(turned[...], d_values[:, :, :, c].reshape(GROUPS * 208, 256)))
            pack_pair(halves[0], halves[1], (first, second)[nb], z, slice(0, 256))
        small = dot(turned[...], d_logits[...].reshape(GROUPS * 208, 128))
        pack_pair(small, jnp.zeros_like(small), first, z, slice(256, 384))
        turned[:, :384] = attended[:, :, :, columns].reshape(384, 256).T
        for nb in range(2):
            halves = []
            for half in range(2):
                c = slice(half * 512 + nb * 256, half * 512 + (nb + 1) * 256)
                halves.append(dot(turned[:, :384], grad[:, :, :, c].reshape(384, 256)))
            pack_pair(halves[0], halves[1], third, z, slice(nb * 256, (nb + 1) * 256))

    looped(4, block, hooks)


def normalise(window, gain, normed):
    for win in range(4):
        values = window(win)
        centred = values - jnp.mean(values, axis=-1, keepdims=True)
        spread = jnp.mean(centred * centred, axis=-1, keepdims=True)
        normed[win * 96 : (win + 1) * 96, :] = (centred * lax.rsqrt(spread + 1e-05) * gain).astype(BF16)


def weight_block(w, layer, block, j):
    tile = layer * 8 + block
    return jnp.concatenate([w[tile + 4 * i, j // 2, j % 2].reshape(D, 128) for i in range(2)], axis=1)


def attend_heads(j, layer, w, normed, bias, mixed):
    queries, keys, values = (dot(normed[...], weight_block(w, layer, block, j)) for block in range(3))
    queries, keys, values = (queries * 0.125).astype(BF16), keys.astype(BF16), values.astype(BF16)
    head = lax.broadcasted_iota(jnp.int32, (96, 256), 1) // 64
    columns = pl.ds(pl.multiple_of(j * 256, 256), 256)
    for win in range(4):
        rows = slice(win * 96, (win + 1) * 96)
        q, k, v = queries[rows], keys[rows], values[rows]
        stacked = jnp.concatenate([jnp.where(head == h, q, jnp.zeros_like(q)) for h in range(4)], axis=0)
        logits = dot(stacked, k, ((1,), (1,)))
        if bias is not None:
            logits = (logits.reshape(4, 96, 96) + bias[win][None]).reshape(384, 96)
        e = jnp.exp(logits - jnp.max(logits, axis=-1, keepdims=True))
        out = dot(e.astype(BF16), v) * (1.0 / jnp.sum(e, axis=-1, keepdims=True))
        total = jnp.zeros((96, 256), F32)
        for h in range(4):
            total = total + jnp.where(head == h, out[h * 96 : (h + 1) * 96], 0.0)
        mixed[rows, columns] = total.astype(BF16)


def output_update(w, layer, j, mixed):
    return dot(mixed[...], weight_block(w, layer, 3, j)).reshape(2, 2, 4, LATENT, 8, 256)


def tile_rows(x, wr, columns=slice(None)):
    return x[4 * wr : 4 * wr + 4, :, :, columns].astype(F32)


def first_sublayer(x, gain, w, normed, mixed, middle, hooks):
    def window(win):
        wr, wc = divmod(win, 2)
        return tile_rows(x, wr)[:, :, 8 * wc : 8 * wc + 8].reshape(96, D)

    normalise(window, gain, normed)
    looped(4, lambda j: attend_heads(j, 0, w, normed, None, mixed), hooks)
    for j in range(4):
        columns = slice(j * 256, (j + 1) * 256)
        update = output_update(w, 0, j, mixed)
        for wr in range(2):
            both = jnp.concatenate([update[wr, 0], update[wr, 1]], axis=2)
            middle[4 * wr : 4 * wr + 4, :, 0:16, columns] = tile_rows(x, wr, columns) + both


def second_sublayer(middle, gain, w, normed, mixed, bias, out, hooks):
    def window(win):
        wr, wc = divmod(win, 2)
        return middle[4 * wr + 2 : 4 * wr + 6, :, 8 * wc + 4 : 8 * wc + 12, :].reshape(96, D)

    normalise(window, gain, normed)
    looped(4, lambda j: attend_heads(j, 1, w, normed, bias, mixed), hooks)
    for j in range(4):
        columns = slice(j * 256, (j + 1) * 256)
        update = output_update(w, 1, j, mixed)
        for wr in range(2):
            halves = []
            for wc in range(2):
                own = middle[4 * wr + 2 : 4 * wr + 6, :, 8 * wc + 4 : 8 * wc + 12, columns]
                halves.append(own + update[wr, wc])
            both = jnp.concatenate(halves, axis=2).astype(BF16)
            out[4 * wr : 4 * wr + 4, :, :, columns] = both


class Edges:
    def __init__(self, place, middle, rows_out, columns_out, rows_in, columns_in, corner_in, send, recv):
        lat, lon = device_of(place)
        above, beside = (lat + 31) % 32, (lon + 3) % 4
        self.middle, self.rows_out, self.columns_out = middle, rows_out, columns_out
        self.rows_in, self.columns_in, self.corner_in = rows_in, columns_in, corner_in
        plan = (
            (rows_out, rows_in, (above, lon)),
            (columns_out, columns_in, (lat, beside)),
            (columns_out.at[pl.ds(0, 32)], corner_in, (above, beside)),
        )
        self.copies = [
            pltpu.make_async_remote_copy(
                src_ref=src,
                dst_ref=dst,
                send_sem=send.at[k],
                recv_sem=recv.at[k],
                device_id=other,
                device_id_type=MESH,
            )
            for k, (src, dst, other) in enumerate(plan)
        ]

    def start(self):
        middle = self.middle
        for r in range(2):
            self.rows_out[r] = middle[r, :, 0:16].reshape(48, D).astype(BF16)
        for part in range(6):
            cells = [divmod(part * 4 + i, LATENT) for i in range(4)]
            rows = jnp.concatenate([middle[r, q, 0:4] for r, q in cells], axis=0)
            self.columns_out[part * 16 : (part + 1) * 16] = rows.astype(BF16)
        for copy in self.copies:
            copy.start()

    def finish(self):
        middle = self.middle
        for copy in self.copies:
            copy.wait_recv()
        for r in range(2):
            middle[8 + r, :, 0:16] = self.rows_in[r].astype(F32).reshape(LATENT, 16, D)
        for part in range(6):
            rows = self.columns_in[part * 16 : (part + 1) * 16].astype(F32)
            for i in range(4):
                r, q = divmod(part * 4 + i, LATENT)
                middle[r, q, 16:20] = rows[i * 4 : (i + 1) * 4]
        for part in range(2):
            rows = self.corner_in[part * 16 : (part + 1) * 16].astype(F32)
            for i in range(4):
                r, q = divmod(part * 4 + i, LATENT)
                if r < 2:
                    middle[8 + r, q, 16:20] = rows[i * 4 : (i + 1) * 4]

    def drain(self):
        for copy in self.copies:
            copy.wait_send()


class Tiles:
    def __init__(self, place, latents, x, send, recv, own):
        lat, lon = device_of(place)

        def at(column):
            return pl.ds(pl.multiple_of(column * 16, 16), 16)

        self.own = pltpu.make_async_copy(latents.at[:, :, at(lon)], x.at[pl.ds(2 * lon, 2)], own)
        self.out, self.arriving = [], []
        for k in range(1, 4):
            there, source = (lon + k) % 4, (lon + 4 - k) % 4
            for copies, column, row, other in (
                (self.out, there, lon, there),
                (self.arriving, source, source, source),
            ):
                copies.append(
                    pltpu.make_async_remote_copy(
                        src_ref=latents.at[:, :, at(column)],
                        dst_ref=x.at[pl.ds(2 * row, 2)],
                        send_sem=send.at[k - 1],
                        recv_sem=recv.at[k - 1],
                        device_id=(lat, other),
                        device_id_type=MESH,
                    )
                )

    def start(self):
        for copy in self.out:
            copy.start()
        self.own.start()

    def finish(self):
        self.own.wait()
        for copy in self.arriving:
            copy.wait_recv()

    def drain(self):
        for copy in self.out:
            copy.wait_send()


WIDTHS = (384, 256, 512)
REDUCE_ORDERS = (("x", "y", "z"), ("y", "z", "x"), ("z", "x", "y"))


def kernel(factor, tokens, grads, kw_far, vw_far, ro_far, lq, gains, qkv, ow, bias, *refs):
    out, grad_key, grad_value, grad_out = refs[:4]
    w, latents, x, rows_out, columns_out, rows_in, columns_in, corner_in = refs[4:12]
    packed, landing = refs[12:15], refs[15:54]
    g_send, g_recv, r_send, r_recv, t_send, t_recv, e_send, e_recv, near = refs[54:]
    place = my_place()
    y = place["y"]
    own = []
    for layer in range(2):
        for half in range(2):
            columns = pl.ds(128 * half, 128)
            tile = layer * 8 + half * 4
            mine = (y % 2, place["core"], place["z"], y // 2, place["x"])
            own.append((qkv.at[layer, :, :, columns], w.at[(pl.ds(tile, 3),) + mine]))
            own.append((ow.at[layer, :, columns], w.at[(tile + 3,) + mine]))
    own = [pltpu.make_async_copy(src, dst, near.at[i]) for i, (src, dst) in enumerate(own)]
    for copy in own:
        copy.start()
    layers = [
        [Gather(place, w, g_send, g_recv, 3 * layer + i, part) for i, part in enumerate(PARTS[layer])]
        for layer in range(2)
    ]
    sums = [
        Reduce(place, packed[i], landing[13 * i : 13 * i + 13], r_send.at[i], r_recv.at[i], REDUCE_ORDERS[i])
        for i in range(3)
    ]
    tiles = Tiles(place, latents, x, t_send, t_recv, near.at[8])

    def gathered(layer, s):
        def hook():
            for part in layers[layer]:
                part.step(s)

        return hook

    def reduced(s):
        def hook():
            for part in sums:
                part.step(s)

        return hook

    def both(*hooks):
        def hook():
            for one in hooks:
                one()

        return hook

    def resampler(tok, grad, kw, vw, ro, kq, values, logits, weights, spread, d_att, att, d_logits, turned):
        pairs = ((kw_far, kw), (tokens, tok), (vw_far, vw), (grads, grad), (ro_far, ro))
        copies = [pltpu.make_async_copy(far, here, near.at[9 + i]) for i, (far, here) in enumerate(pairs)]
        for copy in copies:
            copy.start()
        greet(place)
        for copy in own:
            copy.wait()
        gathered(0, 0)()
        gathered(1, 0)()
        spread_heads(spread)
        copies[0].wait()
        key_queries(kw, lq, kq)
        gathered(0, 1)()
        gathered(1, 1)()
        copies[1].wait()
        copies[2].wait()
        gathered(0, 2)()
        hooks = {0: both(gathered(0, 3), gathered(1, 2)), 1: gathered(0, 4)}
        resample_project(tok, vw, kq, values, logits, hooks)
        resample_softmax(logits, weights)
        copies[3].wait()
        copies[4].wait()
        resample_cotangents(grad, ro, d_att)
        hooks = {0: gathered(1, 3), 4: both(gathered(0, 5), gathered(1, 4))}
        resample_mix(values, weights, logits, spread, d_att, att, d_logits, hooks)
        resample_latents(att, ro, lq, latents)
        tiles.start()
        hooks = {0: gathered(0, 6), 3: gathered(0, 7)}
        resample_gradients(tok, grad, att, values, d_logits, turned, packed, hooks)

    pl.run_scoped(
        resampler,
        pltpu.VMEM((2, LEV, 64, D), BF16),
        pltpu.VMEM((2, LATENT, 64, D), BF16),
        pltpu.VMEM((D, D), BF16),
        pltpu.VMEM((D, D), BF16),
        pltpu.VMEM((D, D), BF16),
        pltpu.VMEM((2, D, 128), BF16),
        pltpu.VMEM((2, LEV, 64, D), BF16),
        pltpu.VMEM((2, LEV, 64, 128), F32),
        pltpu.VMEM((2, LEV, 64, 128), BF16),
        pltpu.VMEM((4, 128, 768), BF16),
        pltpu.VMEM((2, LATENT, 64, D), BF16),
        pltpu.VMEM((2, LATENT, 64, D), BF16),
        pltpu.VMEM((2, LEV, 64, 128), BF16),
        pltpu.VMEM((256, GROUPS * 208), BF16),
    )
    reduced(0)()

    def backbone(middle, normed, mixed):
        edges = Edges(place, middle, rows_out, columns_out, rows_in, columns_in, corner_in, e_send, e_recv)
        tiles.finish()
        hooks = {0: reduced(1), 1: gathered(1, 5), 2: reduced(2), 3: gathered(1, 6)}
        first_sublayer(x, gains[0:1, :], w, normed, mixed, middle, hooks)
        edges.start()
        gathered(1, 7)()
        reduced(3)()
        edges.finish()
        hooks = {0: reduced(4), 1: reduced(5), 2: reduced(6), 3: reduced(7)}
        second_sublayer(middle, gains[1:2, :], w, normed, mixed, bias, out, hooks)
        edges.drain()

    pl.run_scoped(
        backbone,
        pltpu.VMEM((10, LATENT, 24, D), F32),
        pltpu.VMEM((384, D), BF16),
        pltpu.VMEM((384, D), BF16),
    )
    finish_gradients(factor, [part.result() for part in sums], lq, grad_key, grad_value, grad_out)
    tiles.drain()
    for part in layers[0] + layers[1] + sums:
        part.drain()


def whole(factor, tokens, grads, kw, vw, ro, lq, gains, qkv, ow, bias):
    vmem, far = pl.BlockSpec(memory_space=pltpu.VMEM), pl.BlockSpec(memory_space=pl.ANY)
    landings = []
    for order, width in zip(REDUCE_ORDERS, WIDTHS):
        landings += landing_shapes(order, width)
    dma = pltpu.SemaphoreType.DMA
    return pl.pallas_call(
        functools.partial(kernel, factor),
        out_shape=[jax.ShapeDtypeStruct((8, LATENT, 16, D), BF16)] + [jax.ShapeDtypeStruct((8, D), F32)] * 3,
        in_specs=[far] * 5 + [vmem, vmem, far, far, vmem],
        out_specs=[vmem] * 4,
        scratch_shapes=[
            pltpu.VMEM((16, 2, 2, 4, 2, 4, 32, 128), BF16),
            pltpu.VMEM((2, LATENT, 64, D), BF16),
            pltpu.VMEM((8, LATENT, 16, D), BF16),
            pltpu.VMEM((2, 48, D), BF16),
            pltpu.VMEM((96, D), BF16),
            pltpu.VMEM((2, 48, D), BF16),
            pltpu.VMEM((96, D), BF16),
            pltpu.VMEM((32, D), BF16),
        ]
        + [pltpu.VMEM((2, 4, 2, 4, 2, 16, width), BF16) for width in WIDTHS]
        + landings
        + [dma((6, 13)), dma((6, 13)), dma((3, 13)), dma((3, 13))]
        + [dma((3,)), dma((3,)), dma((3,)), dma((3,)), dma((14,))],
        compiler_params=pltpu.CompilerParams(collective_id=0, has_side_effects=True, vmem_limit_bytes=63 * MIB),
    )(tokens, grads, kw, vw, ro, lq, gains, qkv, ow, bias)


def hand_over_kernel(*refs):
    count = len(refs) // 2
    for i in range(count):
        refs[count + i][...] = refs[i][...]


def hand_over(results):
    return pl.pallas_call(
        hand_over_kernel,
        out_shape=[jax.ShapeDtypeStruct(r.shape, r.dtype) for r in results],
        in_specs=[pl.BlockSpec(memory_space=pltpu.VMEM)] * len(results),
        out_specs=[pl.BlockSpec(memory_space=pltpu.VMEM)] * len(results),
    )(*results)


def local(
    level_tokens,
    latent_query,
    key_weight,
    value_weight,
    resample_out,
    norm_gain,
    qkv_weight,
    out_weight,
    window_label,
    grad_latents,
):
    row = lax.axis_index("lat") * 8 + jnp.arange(8, dtype=jnp.int32)
    codes = window_label * 2 + (row >= 8 * lax.axis_size("lat") - 2).astype(jnp.int32)[:, None]
    codes = codes.reshape(2, 4, 2, 8).transpose(0, 2, 1, 3)
    codes = jnp.broadcast_to(codes[:, :, :, None], (2, 2, 4, LATENT, 8)).reshape(4, 96)
    bias = jnp.where(codes[:, :, None] == codes[:, None, :], 0.0, -1e30).astype(F32)
    factor = (2 * 64 * lax.axis_size("lat") * lax.axis_size("lon")) ** (-0.5)
    results = whole(
        factor,
        level_tokens.swapaxes(1, 2),
        grad_latents.swapaxes(1, 2),
        key_weight,
        value_weight,
        resample_out,
        latent_query,
        norm_gain,
        qkv_weight.swapaxes(1, 2),
        out_weight,
        bias,
    )
    out, grad_key, grad_value, grad_out = hand_over(results)
    return (out.swapaxes(1, 2), grad_key, grad_value, grad_out)


def solution(mesh):
    in_specs = (
        P(("lat", "lon"), None, None, None),
        P(),
        P(),
        P(),
        P(),
        P(),
        P(None, "lat", None, "lon"),
        P(None, "lat", "lon"),
        P("lat", "lon"),
        P(("lat", "lon"), None, None, None),
    )
    out_specs = (
        P("lat", "lon", None, None),
        P(("lat", "lon"), None),
        P(("lat", "lon"), None),
        P(("lat", "lon"), None),
    )
    return jax.shard_map(local, mesh=mesh, in_specs=in_specs, out_specs=out_specs, check_vma=False)
```

time: 204 us -> 97.7 us (0.48)
  the two profiles are of different devices: /device:TPU:1 before, /device:TPU:0 now
where the time goes in v2:
time: 97.7 us; the launch traced here: 97.5 us
  Pallas kernels  95.1 us (97%)
  other arithmetic  1.56 us (2%)
    pallas_call x1, Pallas kernels, whole(): pl.pallas_call(functools.partial(kernel, factor), out_shape=[jax.ShapeDty...  93 us
    pallas_call x1, Pallas kernels, hand_over(): pl.pallas_call(hand_over_kernel, out_shape=[jax.ShapeDtypeStruct(r.shape,...  2.1 us

profile of v2, /device:TPU:0, one launch (start us, length us, event | category | flops | bytes accessed | tf_op | source)
XLA Modules:
  0.0 97.5 jit_solution(5502112850033430574)
XLA Ops:
  0.6 0.8 multiply_add_fusion
  1.4 0.1 reshape.20
  1.5 0.1 eq.15
  1.6 0.8 compare_select_fusion.bias
  2.4 93.0 %shard_map.129 = (bf16[8,3,16,1024]{3,2,1,0:T(8,128)(2,1)}, f32[8,1024]{1,0:T(8,128)}, f32[8,1024]{1,0:T(8,128)}, f32[8,1024]{1,0:T(8,128)}) custom-call(bf16[2,13,64,1024]{3,2,1,0:T(8,128)(2,1)} %bitcast.5, bf16[2,3,64,1024]{3,2,1,0:T(8,128)(2,1)} %bitcast.6, bf16[1024,1024]{1,0:T(8,128)(2,1)} %kw_far.1, bf16[1024,1024]{1,0:T(8,128)(2,1)} %vw_far.1, ...), custom_call_target="tpu_custom_call" | custom-call | tf_op jit(solution)/shard_map/pallas_call | solution.py:718
  95.4 2.1 %shard_map.130 = (bf16[8,3,16,1024]{3,2,1,0:T(8,128)(2,1)}, f32[8,1024]{1,0:T(8,128)}, f32[8,1024]{1,0:T(8,128)}, f32[8,1024]{1,0:T(8,128)}) custom-call(bf16[8,3,16,1024]{3,2,1,0:T(8,128)(2,1)} %get-tuple-element.12.refs_0_, f32[8,1024]{1,0:T(8,128)} %get-tuple-element.13.refs_1_, f32[8,1024]{1,0:T(8,128)} %get-tuple-element.14.refs_2_, ...), custom_call_target="tpu_custom_call" | custom-call | tf_op jit(solution)/shard_map/pallas_call | solution.py:748
  (3 shorter events, 0.0 us)

commit v3 on v2

--- a/solution.py
+++ b/solution.py
@@ -53,7 +53,7 @@
 
 def greet(place):
     barrier = pltpu.get_barrier_semaphore()
-    others = [moved(place, dim, step) for dim in "xyz" for step in (1, -1)] + [moved(place, "core", 1)]
+    others = [moved(place, dim, step) for dim in "xyz" for step in (1, -1, 2)] + [moved(place, "core", 1)]
     lat, lon = device_of(place)
     others += [(lat, (lon + k) % 4) for k in range(1, 4)]
     others += [((lat + step) % 32, (lon + turn) % 4) for step, turn in ((1, 0), (31, 0), (1, 1), (31, 3))]
@@ -64,7 +64,7 @@
 
 PARTS = (
     ((0, 3, ("x", "y", "z")), (3, 3, ("y", "z", "x")), (6, 2, ("z", "x", "y"))),
-    ((8, 3, ("z", "x", "y")), (11, 3, ("x", "y", "z")), (14, 2, ("y", "z", "x"))),
+    ((8, 3, ("x", "y", "z")), (11, 3, ("y", "z", "x")), (14, 2, ("z", "x", "y"))),
 )
 
 
@@ -74,7 +74,7 @@
         first, count, self.order = part
         self.tiles = pl.ds(first, count)
 
-    def region(self, phase, value, half=None):
+    def region(self, phase, value, half=None, core=None):
         index = {}
         for position, dim in enumerate(self.order):
             if position < phase:
@@ -84,7 +84,7 @@
             else:
                 index.update(pick(dim, self.place[dim]))
         rows = slice(None) if half is None else pl.ds(16 * half, 16)
-        core = self.place["core"]
+        core = self.place["core"] if core is None else core
         return self.w.at[self.tiles, index["yl"], core, index["z"], index["yh"], index["x"], rows, :]
 
     def copy(self, k, ref, other):
@@ -100,6 +100,8 @@
     def ring(self, phase, k):
         dim = self.order[phase]
         me = self.place[dim]
+        if phase < 2:
+            return self.copy(4 * phase + k, self.region(phase, me), moved(self.place, dim, (1, -1, 2)[k]))
         other = moved(self.place, dim, 1 if k % 2 == 0 else -1)
         if k < 2:
             return self.copy(4 * phase + k, self.region(phase, me), other)
@@ -108,38 +110,43 @@
     def arrival(self, phase, k):
         dim = self.order[phase]
         me = self.place[dim]
-        other = moved(self.place, dim, -1 if k % 2 == 0 else 1)
-        if k < 2:
-            return self.copy(4 * phase + k, self.region(phase, (me + 3 + 2 * k) % 4), other)
-        return self.copy(4 * phase + k, self.region(phase, (me + 2) % 4, k - 2), other)
-
-    def across(self, core):
-        return self.copy(12, self.w.at[self.tiles, :, core], moved(self.place, "core", 1))
+        source = (me + (3, 1, 2, 2)[k]) % 4
+        half = k - 2 if phase == 2 and k > 1 else None
+        return self.copy(4 * phase + k, self.region(phase, source, half), moved(self.place, dim, 1))
+
+    def across(self, k, core):
+        ref = self.region(2, (self.place[self.order[2]] + (0, 3, 1, 2)[k]) % 4, None, core)
+        return self.copy(12 + k, ref, moved(self.place, "core", 1))
 
     def step(self, s):
-        phase, part = divmod(s, 2)
-        if part == 0:
-            if phase > 0:
-                self.arrival(phase - 1, 2).wait_recv()
-                self.arrival(phase - 1, 3).wait_recv()
-            if phase < 3:
-                self.ring(phase, 0).start()
-                self.ring(phase, 1).start()
-            else:
-                self.across(self.place["core"]).start()
-        elif phase < 3:
-            self.arrival(phase, 0).wait_recv()
-            self.ring(phase, 2).start()
-            self.arrival(phase, 1).wait_recv()
-            self.ring(phase, 3).start()
+        core = self.place["core"]
+        if s < 3:
+            if s > 0:
+                for k in range(3):
+                    self.arrival(s - 1, k).wait_recv()
+            for k in range(3 if s < 2 else 2):
+                self.ring(s, k).start()
+            if s == 2:
+                self.across(0, core).start()
+        elif s == 3:
+            for k in range(2):
+                self.arrival(2, k).wait_recv()
+                self.ring(2, k + 2).start()
+                self.across(k + 1, core).start()
+        elif s == 4:
+            for k in (2, 3):
+                self.arrival(2, k).wait_recv()
+            self.across(3, core).start()
         else:
-            self.across(1 - self.place["core"]).wait_recv()
+            for k in range(4):
+                self.across(k, 1 - core).wait_recv()
 
     def drain(self):
         for phase in range(3):
-            for k in range(4):
+            for k in range(3 if phase < 2 else 4):
                 self.ring(phase, k).wait_send()
-        self.across(self.place["core"]).wait_send()
+        for k in range(4):
+            self.across(k, self.place["core"]).wait_send()
 
 
 def landing_shape(order, phase, columns):
@@ -150,15 +157,12 @@
     return (sizes["z"], sizes["yh"], sizes["x"], sizes["yl"], 16, columns)
 
 
-HALF = {256: 128, 384: 128, 512: 256}
-
-
 class Reduce:
     def __init__(self, place, p, landing, send, recv, order):
         self.place, self.p, self.landing = place, p, landing
         self.send, self.recv, self.order = send, recv, order
 
-    def region(self, phase, value, part):
+    def region(self, phase, value):
         index = {}
         for position, dim in enumerate(self.order):
             if position < phase:
@@ -167,15 +171,12 @@
                 index.update(pick(dim, value))
             else:
                 index.update(pick(dim, None))
-        width = self.p.shape[-1]
-        cut = HALF[width]
-        columns = {None: slice(None), 0: pl.ds(0, cut), 1: pl.ds(cut, width - cut)}[part]
-        return (self.place["core"], index["z"], index["yh"], index["x"], index["yl"], slice(None), columns)
-
-    def copy(self, k, src, dst, other):
+        return (self.place["core"], index["z"], index["yh"], index["x"], index["yl"])
+
+    def copy(self, k, src, other):
         return pltpu.make_async_remote_copy(
             src_ref=src,
-            dst_ref=dst,
+            dst_ref=self.landing[k],
             send_sem=self.send.at[k],
             recv_sem=self.recv.at[k],
             device_id=other,
@@ -183,54 +184,38 @@
         )
 
     def across(self):
-        return self.copy(12, self.p.at[1 - self.place["core"]], self.landing[12], moved(self.place, "core", 1))
+        return self.copy(9, self.p.at[1 - self.place["core"]], moved(self.place, "core", 1))
 
     def ring(self, phase, k):
         dim = self.order[phase]
-        me = self.place[dim]
-        target = ((me + 2) % 4, (me + 2) % 4, (me + 1) % 4, (me + 3) % 4)[k]
-        part = (0, 1, None, None)[k]
-        other = moved(self.place, dim, 1 if k % 2 == 0 else -1)
-        return self.copy(4 * phase + k, self.p.at[self.region(phase, target, part)], self.landing[4 * phase + k], other)
-
-    def add(self, region, *landed):
-        total = self.p[region].astype(F32)
-        for ref in landed:
-            total = total + ref[...].astype(F32)
-        self.p[region] = total.astype(BF16)
+        step = (1, -1, 2)[k]
+        target = (self.place[dim] + step + 4) % 4
+        return self.copy(3 * phase + k, self.p.at[self.region(phase, target)], moved(self.place, dim, step))
 
     def step(self, s):
         if s == 0:
             self.across().start()
-            return
-        phase, part = divmod(s - 1, 2)
-        land = self.landing
-        if part == 0:
-            if phase == 0:
-                self.across().wait_recv()
-                core = self.place["core"]
-                for z in range(4):
-                    self.p[core, z] = (self.p[core, z].astype(F32) + land[12][z].astype(F32)).astype(BF16)
-            else:
-                self.ring(phase - 1, 2).wait_recv()
-                self.ring(phase - 1, 3).wait_recv()
-                me = self.place[self.order[phase - 1]]
-                self.add(self.region(phase - 1, me, None), land[4 * phase - 2], land[4 * phase - 1])
-            if phase < 3:
-                self.ring(phase, 0).start()
-                self.ring(phase, 1).start()
+        elif s == 1:
+            self.across().wait_recv()
+            core = self.place["core"]
+            for z in range(4):
+                total = self.p[core, z].astype(F32) + self.landing[9][z].astype(F32)
+                self.p[core, z] = total.astype(BF16)
         else:
-            me = self.place[self.order[phase]]
-            self.ring(phase, 0).wait_recv()
-            self.add(self.region(phase, (me + 1) % 4, 0), land[4 * phase])
-            self.ring(phase, 2).start()
-            self.ring(phase, 1).wait_recv()
-            self.add(self.region(phase, (me + 3) % 4, 1), land[4 * phase + 1])
-            self.ring(phase, 3).start()
+            for k in range(3):
+                self.ring(s - 2, k).wait_recv()
+            region = self.region(s - 2, self.place[self.order[s - 2]])
+            total = self.p[region].astype(F32)
+            for k in range(3):
+                total = total + self.landing[3 * (s - 2) + k][...].astype(F32)
+            self.p[region] = total.astype(BF16)
+        if 0 < s < 4:
+            for k in range(3):
+                self.ring(s - 1, k).start()
 
     def drain(self):
         for phase in range(3):
-            for k in range(4):
+            for k in range(3):
                 self.ring(phase, k).wait_send()
         self.across().wait_send()
 
@@ -240,12 +225,8 @@
 
 
 def landing_shapes(order, columns):
-    shapes = []
-    for phase in range(3):
-        for part in (HALF[columns], columns - HALF[columns], columns, columns):
-            shapes.append(pltpu.VMEM(landing_shape(order, phase, part), BF16))
-    shapes.append(pltpu.VMEM((4, 2, 4, 2, 16, columns), BF16))
-    return shapes
+    shapes = [pltpu.VMEM(landing_shape(order, phase, columns), BF16) for phase in range(3) for _ in range(3)]
+    return shapes + [pltpu.VMEM((4, 2, 4, 2, 16, columns), BF16)]
 
 
 def spread_queries(lq):
@@ -340,9 +321,10 @@
         d_attended[:, :, :, columns] = part.astype(BF16).reshape(2, LATENT, 64, 256)
 
 
-def resample_mix(values, weights, probs, spread, d_attended, attended, d_logits, hooks):
+def resample_mix(chip, values, weights, probs, spread, d_attended, attended, d_logits, hooks):
     def group(g):
-        r, c = group_at(g)
+        r, tile = g % 2, ((chip + 1 + g // 4) % 2) * 2 + (g // 2) % 2
+        c = pl.ds(pl.multiple_of(tile * 16, 16), 16)
         w = weights[r, :, c].reshape(208, 128)
         d_weights = jnp.zeros((208, 128), F32)
         for cb in range(4):
@@ -366,13 +348,14 @@
     looped(GROUPS, group, hooks)
 
 
-def resample_latents(attended, ro, lq, latents):
-    rows = attended[...].reshape(384, D)
+def resample_latents(chip, attended, ro, lq, latents):
+    cells = pl.ds(pl.multiple_of(chip * 32, 32), 32)
+    rows = attended[:, :, cells, :].reshape(192, D)
     for nb in range(4):
         columns = slice(nb * 256, (nb + 1) * 256)
-        part = dot(rows, ro[:, columns]).reshape(2, LATENT, 64, 256)
+        part = dot(rows, ro[:, columns]).reshape(2, LATENT, 32, 256)
         part = part + lq[:, columns].astype(F32)[None, :, None, :]
-        latents[:, :, :, columns] = part.astype(BF16)
+        latents[:, :, cells, columns] = part.astype(BF16)
 
 
 def pack_pair(left, right, p, z, columns):
@@ -383,9 +366,21 @@
         p[core, z, :, :, :, :, columns] = both.astype(BF16)
 
 
-def resample_gradients(tok, grad, attended, d_values, d_logits, turned, packed, hooks):
-    first, second, third = packed
-
+def out_gradient(grad, attended, turned, packed):
+    def block(z):
+        columns = pl.ds(pl.multiple_of(z * 256, 256), 256)
+        turned[:, :384] = attended[:, :, :, columns].reshape(384, 256).T
+        for nb in range(2):
+            halves = []
+            for half in range(2):
+                c = slice(half * 512 + nb * 256, half * 512 + (nb + 1) * 256)
+                halves.append(dot(turned[:, :384], grad[:, :, :, c].reshape(384, 256)))
+            pack_pair(halves[0], halves[1], packed, z, slice(nb * 256, (nb + 1) * 256))
+
+    looped(4, block, {})
+
+
+def token_gradients(tok, d_values, d_logits, turned, packed, hooks):
     def block(z):
         columns = pl.ds(pl.multiple_of(z * 256, 256), 256)
         turned[...] = tok[:, :, :, columns].reshape(GROUPS * 208, 256).T
@@ -394,16 +389,9 @@
             for half in range(2):
                 c = slice(half * 512 + nb * 256, half * 512 + (nb + 1) * 256)
                 halves.append(dot(turned[...], d_values[:, :, :, c].reshape(GROUPS * 208, 256)))
-            pack_pair(halves[0], halves[1], (first, second)[nb], z, slice(0, 256))
+            pack_pair(halves[0], halves[1], packed[nb], z, slice(0, 256))
         small = dot(turned[...], d_logits[...].reshape(GROUPS * 208, 128))
-        pack_pair(small, jnp.zeros_like(small), first, z, slice(256, 384))
-        turned[:, :384] = attended[:, :, :, columns].reshape(384, 256).T
-        for nb in range(2):
-            halves = []
-            for half in range(2):
-                c = slice(half * 512 + nb * 256, half * 512 + (nb + 1) * 256)
-                halves.append(dot(turned[:, :384], grad[:, :, :, c].reshape(384, 256)))
-            pack_pair(halves[0], halves[1], third, z, slice(nb * 256, (nb + 1) * 256))
+        pack_pair(small, jnp.zeros_like(small), packed[0], z, slice(256, 384))
 
     looped(4, block, hooks)
 
@@ -424,21 +412,46 @@
 def attend_heads(j, layer, w, normed, bias, mixed):
     queries, keys, values = (dot(normed[...], weight_block(w, layer, block, j)) for block in range(3))
     queries, keys, values = (queries * 0.125).astype(BF16), keys.astype(BF16), values.astype(BF16)
-    head = lax.broadcasted_iota(jnp.int32, (96, 256), 1) // 64
+    left = lax.broadcasted_iota(jnp.int32, (96, 128), 1) < 64
     columns = pl.ds(pl.multiple_of(j * 256, 256), 256)
+    none = jnp.zeros((96, 128), BF16)
     for win in range(4):
         rows = slice(win * 96, (win + 1) * 96)
         q, k, v = queries[rows], keys[rows], values[rows]
-        stacked = jnp.concatenate([jnp.where(head == h, q, jnp.zeros_like(q)) for h in range(4)], axis=0)
-        logits = dot(stacked, k, ((1,), (1,)))
+        stacked = []
+        for h in range(4):
+            half = q[:, 128 * (h // 2) : 128 * (h // 2 + 1)]
+            half = jnp.where(left, half, none) if h % 2 == 0 else jnp.where(left, none, half)
+            stacked.append(jnp.concatenate([half, none] if h < 2 else [none, half], axis=1))
+        logits = dot(jnp.concatenate(stacked, axis=0), k, ((1,), (1,)))
         if bias is not None:
             logits = (logits.reshape(4, 96, 96) + bias[win][None]).reshape(384, 96)
         e = jnp.exp(logits - jnp.max(logits, axis=-1, keepdims=True))
-        out = dot(e.astype(BF16), v) * (1.0 / jnp.sum(e, axis=-1, keepdims=True))
-        total = jnp.zeros((96, 256), F32)
-        for h in range(4):
-            total = total + jnp.where(head == h, out[h * 96 : (h + 1) * 96], 0.0)
-        mixed[rows, columns] = total.astype(BF16)
+        e = e * (1.0 / jnp.sum(e, axis=-1, keepdims=True))
+        out = dot(e.astype(BF16), v)
+        pairs = [
+            jnp.where(left, out[0:96, :128], out[96:192, :128]),
+            jnp.where(left, out[192:288, 128:], out[288:384, 128:]),
+        ]
+        mixed[rows, columns] = jnp.concatenate(pairs, axis=1).astype(BF16)
+
+
+def label_mask(label, place, bias):
+    lat = device_of(place)[0]
+    row = lax.broadcasted_iota(jnp.int32, (8, 16), 0) + lat * 8
+    codes = label[...].astype(F32) * 2.0 + jnp.where(row >= 8 * 32 - 2, 2.0, 1.0)
+    token = lax.broadcasted_iota(jnp.int32, (96, 16), 0)
+    column = lax.broadcasted_iota(jnp.int32, (96, 16), 1)
+    ones = jnp.ones((96, 16), F32)
+    for win in range(4):
+        wr, wc = divmod(win, 2)
+        own = jnp.zeros((96, 16), F32)
+        for r in range(4):
+            hit = (token // 24 == r) & (column == 8 * wc + token % 8)
+            own = own + jnp.where(hit, codes[4 * wr + r : 4 * wr + r + 1, :], 0.0)
+        one = dot(own, ones, ((1,), (1,)))
+        other = dot(ones, own, ((1,), (1,)))
+        bias[win] = jnp.where(one == other, 0.0, -1e30)
 
 
 def output_update(w, layer, j, mixed):
@@ -548,28 +561,29 @@
             return pl.ds(pl.multiple_of(column * 16, 16), 16)
 
         self.own = pltpu.make_async_copy(latents.at[:, :, at(lon)], x.at[pl.ds(2 * lon, 2)], own)
+        chip, core = lon // 2, lon % 2
+        partners = ((1 - chip) * 2 + core, (1 - chip) * 2 + 1 - core, chip * 2 + 1 - core)
         self.out, self.arriving = [], []
-        for k in range(1, 4):
-            there, source = (lon + k) % 4, (lon + 4 - k) % 4
-            for copies, column, row, other in (
-                (self.out, there, lon, there),
-                (self.arriving, source, source, source),
-            ):
+        for k, other in enumerate(partners):
+            for copies, row in ((self.out, lon), (self.arriving, other)):
                 copies.append(
                     pltpu.make_async_remote_copy(
-                        src_ref=latents.at[:, :, at(column)],
+                        src_ref=latents.at[:, :, at(other)],
                         dst_ref=x.at[pl.ds(2 * row, 2)],
-                        send_sem=send.at[k - 1],
-                        recv_sem=recv.at[k - 1],
+                        send_sem=send.at[k],
+                        recv_sem=recv.at[k],
                         device_id=(lat, other),
                         device_id_type=MESH,
                     )
                 )
 
-    def start(self):
-        for copy in self.out:
-            copy.start()
-        self.own.start()
+    def start(self, here):
+        if here:
+            self.out[2].start()
+            self.own.start()
+        else:
+            self.out[0].start()
+            self.out[1].start()
 
     def finish(self):
         self.own.wait()
@@ -585,11 +599,11 @@
 REDUCE_ORDERS = (("x", "y", "z"), ("y", "z", "x"), ("z", "x", "y"))
 
 
-def kernel(factor, tokens, grads, kw_far, vw_far, ro_far, lq, gains, qkv, ow, bias, *refs):
+def kernel(factor, tokens, grads, kw_far, vw_far, ro_far, lq, gains, qkv, ow, label, *refs):
     out, grad_key, grad_value, grad_out = refs[:4]
     w, latents, x, rows_out, columns_out, rows_in, columns_in, corner_in = refs[4:12]
-    packed, landing = refs[12:15], refs[15:54]
-    g_send, g_recv, r_send, r_recv, t_send, t_recv, e_send, e_recv, near = refs[54:]
+    packed, landing = refs[12:15], refs[15:45]
+    g_send, g_recv, r_send, r_recv, t_send, t_recv, e_send, e_recv, near = refs[45:]
     place = my_place()
     y = place["y"]
     own = []
@@ -608,7 +622,7 @@
         for layer in range(2)
     ]
     sums = [
-        Reduce(place, packed[i], landing[13 * i : 13 * i + 13], r_send.at[i], r_recv.at[i], REDUCE_ORDERS[i])
+        Reduce(place, packed[i], landing[10 * i : 10 * i + 10], r_send.at[i], r_recv.at[i], REDUCE_ORDERS[i])
         for i in range(3)
     ]
     tiles = Tiles(place, latents, x, t_send, t_recv, near.at[8])
@@ -620,10 +634,10 @@
 
         return hook
 
-    def reduced(s):
+    def reduced(s, *parts):
         def hook():
-            for part in sums:
-                part.step(s)
+            for part in parts:
+                sums[part].step(s)
 
         return hook
 
@@ -648,22 +662,27 @@
         copies[0].wait()
         key_queries(kw, lq, kq)
         gathered(0, 1)()
-        gathered(1, 1)()
         copies[1].wait()
         copies[2].wait()
-        gathered(0, 2)()
-        hooks = {0: both(gathered(0, 3), gathered(1, 2)), 1: gathered(0, 4)}
-        resample_project(tok, vw, kq, values, logits, hooks)
+        resample_project(tok, vw, kq, values, logits, {1: gathered(0, 2)})
         resample_softmax(logits, weights)
         copies[3].wait()
         copies[4].wait()
         resample_cotangents(grad, ro, d_att)
-        hooks = {0: gathered(1, 3), 4: both(gathered(0, 5), gathered(1, 4))}
-        resample_mix(values, weights, logits, spread, d_att, att, d_logits, hooks)
-        resample_latents(att, ro, lq, latents)
-        tiles.start()
-        hooks = {0: gathered(0, 6), 3: gathered(0, 7)}
-        resample_gradients(tok, grad, att, values, d_logits, turned, packed, hooks)
+        chip = y % 2
+
+        def first_half():
+            resample_latents(1 - chip, att, ro, lq, latents)
+            tiles.start(False)
+
+        hooks = {1: gathered(1, 1), 3: first_half, 7: gathered(0, 3)}
+        resample_mix(chip, values, weights, logits, spread, d_att, att, d_logits, hooks)
+        resample_latents(chip, att, ro, lq, latents)
+        tiles.start(True)
+        out_gradient(grad, att, turned, packed[2])
+        gathered(1, 2)()
+        reduced(0, 2)()
+        token_gradients(tok, values, d_logits, turned, packed, {1: gathered(0, 4), 2: reduced(1, 2)})
 
     pl.run_scoped(
         resampler,
@@ -682,19 +701,22 @@
         pltpu.VMEM((2, LEV, 64, 128), BF16),
         pltpu.VMEM((256, GROUPS * 208), BF16),
     )
-    reduced(0)()
-
-    def backbone(middle, normed, mixed):
+    reduced(0, 0, 1)()
+
+    def backbone(middle, normed, mixed, bias):
         edges = Edges(place, middle, rows_out, columns_out, rows_in, columns_in, corner_in, e_send, e_recv)
+        label_mask(label, place, bias)
+        gathered(0, 5)()
         tiles.finish()
-        hooks = {0: reduced(1), 1: gathered(1, 5), 2: reduced(2), 3: gathered(1, 6)}
-        first_sublayer(x, gains[0:1, :], w, normed, mixed, middle, hooks)
+        first_sublayer(x, gains[0:1, :], w, normed, mixed, middle, {2: reduced(1, 0, 1), 3: gathered(1, 3)})
         edges.start()
-        gathered(1, 7)()
-        reduced(3)()
+        reduced(2, 2)()
+        gathered(1, 4)()
         edges.finish()
-        hooks = {0: reduced(4), 1: reduced(5), 2: reduced(6), 3: reduced(7)}
+        gathered(1, 5)()
+        hooks = {0: reduced(2, 0, 1), 1: reduced(3, 2), 2: reduced(3, 0, 1), 3: reduced(4, 2)}
         second_sublayer(middle, gains[1:2, :], w, normed, mixed, bias, out, hooks)
+        reduced(4, 0, 1)()
         edges.drain()
 
     pl.run_scoped(
@@ -702,6 +724,7 @@
         pltpu.VMEM((10, LATENT, 24, D), F32),
         pltpu.VMEM((384, D), BF16),
         pltpu.VMEM((384, D), BF16),
+        pltpu.VMEM((4, 96, 96), F32),
     )
     finish_gradients(factor, [part.result() for part in sums], lq, grad_key, grad_value, grad_out)
     tiles.drain()
@@ -709,7 +732,7 @@
         part.drain()
 
 
-def whole(factor, tokens, grads, kw, vw, ro, lq, gains, qkv, ow, bias):
+def whole(factor, tokens, grads, kw, vw, ro, lq, gains, qkv, ow, label):
     vmem, far = pl.BlockSpec(memory_space=pltpu.VMEM), pl.BlockSpec(memory_space=pl.ANY)
     landings = []
     for order, width in zip(REDUCE_ORDERS, WIDTHS):
@@ -732,10 +755,10 @@
         ]
         + [pltpu.VMEM((2, 4, 2, 4, 2, 16, width), BF16) for width in WIDTHS]
         + landings
-        + [dma((6, 13)), dma((6, 13)), dma((3, 13)), dma((3, 13))]
+        + [dma((6, 16)), dma((6, 16)), dma((3, 10)), dma((3, 10))]
         + [dma((3,)), dma((3,)), dma((3,)), dma((3,)), dma((14,))],
         compiler_params=pltpu.CompilerParams(collective_id=0, has_side_effects=True, vmem_limit_bytes=63 * MIB),
-    )(tokens, grads, kw, vw, ro, lq, gains, qkv, ow, bias)
+    )(tokens, grads, kw, vw, ro, lq, gains, qkv, ow, label)
 
 
 def hand_over_kernel(*refs):
@@ -765,11 +788,6 @@
     window_label,
     grad_latents,
 ):
-    row = lax.axis_index("lat") * 8 + jnp.arange(8, dtype=jnp.int32)
-    codes = window_label * 2 + (row >= 8 * lax.axis_size("lat") - 2).astype(jnp.int32)[:, None]
-    codes = codes.reshape(2, 4, 2, 8).transpose(0, 2, 1, 3)
-    codes = jnp.broadcast_to(codes[:, :, :, None], (2, 2, 4, LATENT, 8)).reshape(4, 96)
-    bias = jnp.where(codes[:, :, None] == codes[:, None, :], 0.0, -1e30).astype(F32)
     factor = (2 * 64 * lax.axis_size("lat") * lax.axis_size("lon")) ** (-0.5)
     results = whole(
         factor,
@@ -782,7 +800,7 @@
         norm_gain,
         qkv_weight.swapaxes(1, 2),
         out_weight,
-        bias,
+        window_label,
     )
     out, grad_key, grad_value, grad_out = hand_over(results)
     return (out.swapaxes(1, 2), grad_key, grad_value, grad_out)

time: 97.7 us -> 92.1 us (0.943)
  the two profiles are of different devices: /device:TPU:0 before, /device:TPU:1 now
where the time goes in v3:
time: 92.1 us; the launch traced here: 91.9 us
  Pallas kernels  91.3 us (99%)
    pallas_call x1, Pallas kernels, whole(): pl.pallas_call(functools.partial(kernel, factor), out_shape=[jax.ShapeDty...  89.2 us
    pallas_call x1, Pallas kernels, hand_over(): pl.pallas_call(hand_over_kernel, out_shape=[jax.ShapeDtypeStruct(r.shape,...  2.1 us

profile of v3, /device:TPU:1, one launch (start us, length us, event | category | flops | bytes accessed | tf_op | source)
XLA Modules:
  0.0 91.9 jit_solution(3951181333158500594)
XLA Ops:
  0.6 89.2 %shard_map.129 = (bf16[8,3,16,1024]{3,2,1,0:T(8,128)(2,1)}, f32[8,1024]{1,0:T(8,128)}, f32[8,1024]{1,0:T(8,128)}, f32[8,1024]{1,0:T(8,128)}) custom-call(bf16[2,13,64,1024]{3,2,1,0:T(8,128)(2,1)} %bitcast.4, bf16[2,3,64,1024]{3,2,1,0:T(8,128)(2,1)} %bitcast.5, bf16[1024,1024]{1,0:T(8,128)(2,1)} %kw_far.1, bf16[1024,1024]{1,0:T(8,128)(2,1)} %vw_far.1, ...), custom_call_target="tpu_custom_call" | custom-call | tf_op jit(solution)/shard_map/pallas_call | solution.py:741
  89.8 2.1 %shard_map.130 = (bf16[8,3,16,1024]{3,2,1,0:T(8,128)(2,1)}, f32[8,1024]{1,0:T(8,128)}, f32[8,1024]{1,0:T(8,128)}, f32[8,1024]{1,0:T(8,128)}) custom-call(bf16[8,3,16,1024]{3,2,1,0:T(8,128)(2,1)} %get-tuple-element.12.refs_0_, f32[8,1024]{1,0:T(8,128)} %get-tuple-element.13.refs_1_, f32[8,1024]{1,0:T(8,128)} %get-tuple-element.14.refs_2_, ...), custom_call_target="tpu_custom_call" | custom-call | tf_op jit(solution)/shard_map/pallas_call | solution.py:771

commit v4 on v3

--- a/solution.py
+++ b/solution.py
@@ -462,13 +462,18 @@
     return x[4 * wr : 4 * wr + 4, :, :, columns].astype(F32)
 
 
-def first_sublayer(x, gain, w, normed, mixed, middle, hooks):
+def own_first(i, core):
+    return (i % 2) * 2 + (core + i // 2) % 2
+
+
+def first_sublayer(core, x, gain, w, normed, mixed, middle, ready, hooks):
     def window(win):
         wr, wc = divmod(win, 2)
         return tile_rows(x, wr)[:, :, 8 * wc : 8 * wc + 8].reshape(96, D)
 
     normalise(window, gain, normed)
-    looped(4, lambda j: attend_heads(j, 0, w, normed, None, mixed), hooks)
+    ready()
+    looped(4, lambda i: attend_heads(own_first(i, core), 0, w, normed, None, mixed), hooks)
     for j in range(4):
         columns = slice(j * 256, (j + 1) * 256)
         update = output_update(w, 0, j, mixed)
@@ -477,13 +482,13 @@
             middle[4 * wr : 4 * wr + 4, :, 0:16, columns] = tile_rows(x, wr, columns) + both
 
 
-def second_sublayer(middle, gain, w, normed, mixed, bias, out, hooks):
+def second_sublayer(core, middle, gain, w, normed, mixed, bias, out, hooks):
     def window(win):
         wr, wc = divmod(win, 2)
         return middle[4 * wr + 2 : 4 * wr + 6, :, 8 * wc + 4 : 8 * wc + 12, :].reshape(96, D)
 
     normalise(window, gain, normed)
-    looped(4, lambda j: attend_heads(j, 1, w, normed, bias, mixed), hooks)
+    looped(4, lambda i: attend_heads(own_first(i, core), 1, w, normed, bias, mixed), hooks)
     for j in range(4):
         columns = slice(j * 256, (j + 1) * 256)
         update = output_update(w, 1, j, mixed)
@@ -596,7 +601,7 @@
 
 
 WIDTHS = (384, 256, 512)
-REDUCE_ORDERS = (("x", "y", "z"), ("y", "z", "x"), ("z", "x", "y"))
+REDUCE_ORDERS = (("z", "x", "y"), ("x", "y", "z"), ("y", "z", "x"))
 
 
 def kernel(factor, tokens, grads, kw_far, vw_far, ro_far, lq, gains, qkv, ow, label, *refs):
@@ -657,14 +662,14 @@
         for copy in own:
             copy.wait()
         gathered(0, 0)()
+        spread_heads(spread)
         gathered(1, 0)()
-        spread_heads(spread)
         copies[0].wait()
         key_queries(kw, lq, kq)
         gathered(0, 1)()
         copies[1].wait()
         copies[2].wait()
-        resample_project(tok, vw, kq, values, logits, {1: gathered(0, 2)})
+        resample_project(tok, vw, kq, values, logits, {0: gathered(1, 1)})
         resample_softmax(logits, weights)
         copies[3].wait()
         copies[4].wait()
@@ -675,14 +680,13 @@
             resample_latents(1 - chip, att, ro, lq, latents)
             tiles.start(False)
 
-        hooks = {1: gathered(1, 1), 3: first_half, 7: gathered(0, 3)}
+        hooks = {0: gathered(0, 2), 3: first_half, 6: both(gathered(0, 3), gathered(1, 2))}
         resample_mix(chip, values, weights, logits, spread, d_att, att, d_logits, hooks)
         resample_latents(chip, att, ro, lq, latents)
         tiles.start(True)
         out_gradient(grad, att, turned, packed[2])
-        gathered(1, 2)()
         reduced(0, 2)()
-        token_gradients(tok, values, d_logits, turned, packed, {1: gathered(0, 4), 2: reduced(1, 2)})
+        token_gradients(tok, values, d_logits, turned, packed, {})
 
     pl.run_scoped(
         resampler,
@@ -702,21 +706,25 @@
         pltpu.VMEM((256, GROUPS * 208), BF16),
     )
     reduced(0, 0, 1)()
+    reduced(1, 2)()
 
     def backbone(middle, normed, mixed, bias):
         edges = Edges(place, middle, rows_out, columns_out, rows_in, columns_in, corner_in, e_send, e_recv)
+        core = place["core"]
         label_mask(label, place, bias)
-        gathered(0, 5)()
+        reduced(1, 1)()
         tiles.finish()
-        first_sublayer(x, gains[0:1, :], w, normed, mixed, middle, {2: reduced(1, 0, 1), 3: gathered(1, 3)})
+        ready = both(gathered(0, 4), reduced(1, 0))
+        hooks = {1: gathered(0, 5), 2: gathered(1, 3)}
+        first_sublayer(core, x, gains[0:1, :], w, normed, mixed, middle, ready, hooks)
         edges.start()
+        gathered(1, 4)()
+        reduced(2, 0, 1)()
+        edges.finish()
         reduced(2, 2)()
-        gathered(1, 4)()
-        edges.finish()
-        gathered(1, 5)()
-        hooks = {0: reduced(2, 0, 1), 1: reduced(3, 2), 2: reduced(3, 0, 1), 3: reduced(4, 2)}
-        second_sublayer(middle, gains[1:2, :], w, normed, mixed, bias, out, hooks)
-        reduced(4, 0, 1)()
+        hooks = {1: both(gathered(1, 5), reduced(3, 0, 1)), 2: reduced(3, 2)}
+        second_sublayer(core, middle, gains[1:2, :], w, normed, mixed, bias, out, hooks)
+        reduced(4, 0, 1, 2)()
         edges.drain()
 
     pl.run_scoped(

time: 92.1 us -> 83.9 us (0.911)
  Pallas kernels: 91.3 us -> 83.1 us
    pallas_call x1, Pallas kernels: 89.2 us -> 81 us  [whole(): pl.pallas_call(functools.partial(kernel, factor), out_shape=[jax.ShapeDty...]
where the time goes in v4:
time: 83.9 us; the launch traced here: 83.7 us
  Pallas kernels  83.1 us (99%)
    pallas_call x1, Pallas kernels, whole(): pl.pallas_call(functools.partial(kernel, factor), out_shape=[jax.ShapeDty...  81 us
    pallas_call x1, Pallas kernels, hand_over(): pl.pallas_call(hand_over_kernel, out_shape=[jax.ShapeDtypeStruct(r.shape,...  2.1 us

profile of v4, /device:TPU:1, one launch (start us, length us, event | category | flops | bytes accessed | tf_op | source)
XLA Modules:
  0.0 83.7 jit_solution(12849314324295695976)
XLA Ops:
  0.6 81.0 %shard_map.129 = (bf16[8,3,16,1024]{3,2,1,0:T(8,128)(2,1)}, f32[8,1024]{1,0:T(8,128)}, f32[8,1024]{1,0:T(8,128)}, f32[8,1024]{1,0:T(8,128)}) custom-call(bf16[2,13,64,1024]{3,2,1,0:T(8,128)(2,1)} %bitcast.4, bf16[2,3,64,1024]{3,2,1,0:T(8,128)(2,1)} %bitcast.5, bf16[1024,1024]{1,0:T(8,128)(2,1)} %kw_far.1, bf16[1024,1024]{1,0:T(8,128)(2,1)} %vw_far.1, ...), custom_call_target="tpu_custom_call" | custom-call | tf_op jit(solution)/shard_map/pallas_call | solution.py:749
  81.6 2.1 %shard_map.130 = (bf16[8,3,16,1024]{3,2,1,0:T(8,128)(2,1)}, f32[8,1024]{1,0:T(8,128)}, f32[8,1024]{1,0:T(8,128)}, f32[8,1024]{1,0:T(8,128)}) custom-call(bf16[8,3,16,1024]{3,2,1,0:T(8,128)(2,1)} %get-tuple-element.12.refs_0_, f32[8,1024]{1,0:T(8,128)} %get-tuple-element.13.refs_1_, f32[8,1024]{1,0:T(8,128)} %get-tuple-element.14.refs_2_, ...), custom_call_target="tpu_custom_call" | custom-call | tf_op jit(solution)/shard_map/pallas_call | solution.py:779

commit v5 on v4

--- a/solution.py
+++ b/solution.py
@@ -63,9 +63,12 @@
 
 
 PARTS = (
-    ((0, 3, ("x", "y", "z")), (3, 3, ("y", "z", "x")), (6, 2, ("z", "x", "y"))),
-    ((8, 3, ("x", "y", "z")), (11, 3, ("y", "z", "x")), (14, 2, ("z", "x", "y"))),
+    ((0, 2, ("x", "y", "z")), (2, 2, ("y", "z", "x")), (4, 2, ("z", "x", "y"))),
+    ((6, 1, ("x", "y", "z")), (7, 1, ("y", "z", "x"))),
+    ((8, 2, ("x", "y", "z")), (10, 2, ("y", "z", "x")), (12, 2, ("z", "x", "y"))),
+    ((14, 1, ("y", "z", "x")), (15, 1, ("x", "y", "z"))),
 )
+Q0, O0, Q1, O1 = range(4)
 
 
 class Gather:
@@ -405,8 +408,8 @@
 
 
 def weight_block(w, layer, block, j):
-    tile = layer * 8 + block
-    return jnp.concatenate([w[tile + 4 * i, j // 2, j % 2].reshape(D, 128) for i in range(2)], axis=1)
+    tile = layer * 8 + block * 2
+    return jnp.concatenate([w[tile + i, j // 2, j % 2].reshape(D, 128) for i in range(2)], axis=1)
 
 
 def attend_heads(j, layer, w, normed, bias, mixed):
@@ -466,13 +469,12 @@
     return (i % 2) * 2 + (core + i // 2) % 2
 
 
-def first_sublayer(core, x, gain, w, normed, mixed, middle, ready, hooks):
+def first_sublayer(core, x, gain, w, normed, mixed, middle, hooks):
     def window(win):
         wr, wc = divmod(win, 2)
         return tile_rows(x, wr)[:, :, 8 * wc : 8 * wc + 8].reshape(96, D)
 
     normalise(window, gain, normed)
-    ready()
     looped(4, lambda i: attend_heads(own_first(i, core), 0, w, normed, None, mixed), hooks)
     for j in range(4):
         columns = slice(j * 256, (j + 1) * 256)
@@ -482,12 +484,13 @@
             middle[4 * wr : 4 * wr + 4, :, 0:16, columns] = tile_rows(x, wr, columns) + both
 
 
-def second_sublayer(core, middle, gain, w, normed, mixed, bias, out, hooks):
+def second_sublayer(core, middle, gain, w, normed, mixed, bias, out, ready, hooks):
     def window(win):
         wr, wc = divmod(win, 2)
         return middle[4 * wr + 2 : 4 * wr + 6, :, 8 * wc + 4 : 8 * wc + 12, :].reshape(96, D)
 
     normalise(window, gain, normed)
+    ready()
     looped(4, lambda i: attend_heads(own_first(i, core), 1, w, normed, bias, mixed), hooks)
     for j in range(4):
         columns = slice(j * 256, (j + 1) * 256)
@@ -612,29 +615,28 @@
     place = my_place()
     y = place["y"]
     own = []
-    for layer in range(2):
-        for half in range(2):
-            columns = pl.ds(128 * half, 128)
-            tile = layer * 8 + half * 4
-            mine = (y % 2, place["core"], place["z"], y // 2, place["x"])
-            own.append((qkv.at[layer, :, :, columns], w.at[(pl.ds(tile, 3),) + mine]))
-            own.append((ow.at[layer, :, columns], w.at[(tile + 3,) + mine]))
+    mine = (y % 2, place["core"], place["z"], y // 2, place["x"])
+    for tile in range(16):
+        layer, block, half = tile // 8, tile // 2 % 4, tile % 2
+        columns = pl.ds(128 * half, 128)
+        src = ow.at[layer, :, columns] if block == 3 else qkv.at[layer, block, :, columns]
+        own.append((src, w.at[(tile,) + mine]))
     own = [pltpu.make_async_copy(src, dst, near.at[i]) for i, (src, dst) in enumerate(own)]
     for copy in own:
         copy.start()
-    layers = [
-        [Gather(place, w, g_send, g_recv, 3 * layer + i, part) for i, part in enumerate(PARTS[layer])]
-        for layer in range(2)
-    ]
+    weights_in = []
+    for group in PARTS:
+        first = sum(len(g) for g in weights_in)
+        weights_in.append([Gather(place, w, g_send, g_recv, first + i, part) for i, part in enumerate(group)])
     sums = [
         Reduce(place, packed[i], landing[10 * i : 10 * i + 10], r_send.at[i], r_recv.at[i], REDUCE_ORDERS[i])
         for i in range(3)
     ]
-    tiles = Tiles(place, latents, x, t_send, t_recv, near.at[8])
-
-    def gathered(layer, s):
+    tiles = Tiles(place, latents, x, t_send, t_recv, near.at[16])
+
+    def gathered(group, s):
         def hook():
-            for part in layers[layer]:
+            for part in weights_in[group]:
                 part.step(s)
 
         return hook
@@ -655,21 +657,21 @@
 
     def resampler(tok, grad, kw, vw, ro, kq, values, logits, weights, spread, d_att, att, d_logits, turned):
         pairs = ((kw_far, kw), (tokens, tok), (vw_far, vw), (grads, grad), (ro_far, ro))
-        copies = [pltpu.make_async_copy(far, here, near.at[9 + i]) for i, (far, here) in enumerate(pairs)]
+        copies = [pltpu.make_async_copy(far, here, near.at[17 + i]) for i, (far, here) in enumerate(pairs)]
         for copy in copies:
             copy.start()
         greet(place)
         for copy in own:
             copy.wait()
-        gathered(0, 0)()
+        gathered(Q0, 0)()
         spread_heads(spread)
-        gathered(1, 0)()
+        both(gathered(O0, 0), gathered(Q1, 0), gathered(O1, 0))()
         copies[0].wait()
         key_queries(kw, lq, kq)
-        gathered(0, 1)()
+        gathered(Q0, 1)()
         copies[1].wait()
         copies[2].wait()
-        resample_project(tok, vw, kq, values, logits, {0: gathered(1, 1)})
+        resample_project(tok, vw, kq, values, logits, {0: gathered(Q1, 1), 1: gathered(Q0, 2)})
         resample_softmax(logits, weights)
         copies[3].wait()
         copies[4].wait()
@@ -680,13 +682,14 @@
             resample_latents(1 - chip, att, ro, lq, latents)
             tiles.start(False)
 
-        hooks = {0: gathered(0, 2), 3: first_half, 6: both(gathered(0, 3), gathered(1, 2))}
+        hooks = {1: gathered(O0, 1), 3: both(gathered(O0, 2), gathered(O1, 1), first_half), 7: gathered(Q0, 3)}
         resample_mix(chip, values, weights, logits, spread, d_att, att, d_logits, hooks)
         resample_latents(chip, att, ro, lq, latents)
         tiles.start(True)
         out_gradient(grad, att, turned, packed[2])
-        reduced(0, 2)()
-        token_gradients(tok, values, d_logits, turned, packed, {})
+        gathered(O0, 3)()
+        hooks = {0: gathered(O1, 2), 1: reduced(0, 2), 2: gathered(Q1, 2)}
+        token_gradients(tok, values, d_logits, turned, packed, hooks)
 
     pl.run_scoped(
         resampler,
@@ -712,18 +715,19 @@
         edges = Edges(place, middle, rows_out, columns_out, rows_in, columns_in, corner_in, e_send, e_recv)
         core = place["core"]
         label_mask(label, place, bias)
-        reduced(1, 1)()
+        both(gathered(Q0, 4), gathered(O1, 3), reduced(1, 0, 1))()
         tiles.finish()
-        ready = both(gathered(0, 4), reduced(1, 0))
-        hooks = {1: gathered(0, 5), 2: gathered(1, 3)}
-        first_sublayer(core, x, gains[0:1, :], w, normed, mixed, middle, ready, hooks)
+        hooks = {1: both(gathered(Q0, 5), gathered(O0, 4)), 3: gathered(O0, 5)}
+        first_sublayer(core, x, gains[0:1, :], w, normed, mixed, middle, hooks)
+        gathered(Q1, 3)()
         edges.start()
-        gathered(1, 4)()
-        reduced(2, 0, 1)()
+        gathered(O1, 4)()
+        reduced(2, 2)()
         edges.finish()
-        reduced(2, 2)()
-        hooks = {1: both(gathered(1, 5), reduced(3, 0, 1)), 2: reduced(3, 2)}
-        second_sublayer(core, middle, gains[1:2, :], w, normed, mixed, bias, out, hooks)
+        reduced(2, 1)()
+        ready = both(gathered(Q1, 4), reduced(2, 0))
+        hooks = {1: both(gathered(Q1, 5), reduced(3, 2)), 2: reduced(3, 0, 1), 3: gathered(O1, 5)}
+        second_sublayer(core, middle, gains[1:2, :], w, normed, mixed, bias, out, ready, hooks)
         reduced(4, 0, 1, 2)()
         edges.drain()
 
@@ -736,8 +740,9 @@
     )
     finish_gradients(factor, [part.result() for part in sums], lq, grad_key, grad_value, grad_out)
     tiles.drain()
-    for part in layers[0] + layers[1] + sums:
-        part.drain()
+    for group in weights_in + [sums]:
+        for part in group:
+            part.drain()
 
 
 def whole(factor, tokens, grads, kw, vw, ro, lq, gains, qkv, ow, label):
@@ -763,24 +768,29 @@
         ]
         + [pltpu.VMEM((2, 4, 2, 4, 2, 16, width), BF16) for width in WIDTHS]
         + landings
-        + [dma((6, 16)), dma((6, 16)), dma((3, 10)), dma((3, 10))]
-        + [dma((3,)), dma((3,)), dma((3,)), dma((3,)), dma((14,))],
+        + [dma((10, 16)), dma((10, 16)), dma((3, 10)), dma((3, 10))]
+        + [dma((3,)), dma((3,)), dma((3,)), dma((3,)), dma((22,))],
         compiler_params=pltpu.CompilerParams(collective_id=0, has_side_effects=True, vmem_limit_bytes=63 * MIB),
     )(tokens, grads, kw, vw, ro, lq, gains, qkv, ow, label)
 
 
-def hand_over_kernel(*refs):
-    count = len(refs) // 2
-    for i in range(count):
-        refs[count + i][...] = refs[i][...]
+def hand_over_kernel(tile, *refs):
+    refs[3][...] = tile[...]
+
+    @pl.when(pl.program_id(0) == 0)
+    def _():
+        for i in range(3):
+            refs[4 + i][...] = refs[i][...]
 
 
 def hand_over(results):
+    specs = [pl.BlockSpec((2, LATENT, 16, D), lambda i: (i, 0, 0, 0))] + [pl.BlockSpec((8, D), lambda i: (0, 0))] * 3
     return pl.pallas_call(
         hand_over_kernel,
+        grid=(4,),
         out_shape=[jax.ShapeDtypeStruct(r.shape, r.dtype) for r in results],
-        in_specs=[pl.BlockSpec(memory_space=pltpu.VMEM)] * len(results),
-        out_specs=[pl.BlockSpec(memory_space=pltpu.VMEM)] * len(results),
+        in_specs=specs,
+        out_specs=specs,
     )(*results)
 
 

time: 83.9 us -> 86.4 us (1.030)
  Pallas kernels: 83.1 us -> 84.7 us
    pallas_call x1, Pallas kernels: 2.1 us -> 3.31 us  [hand_over(): pl.pallas_call(hand_over_kernel, grid=(4,), out_shape=[jax.ShapeDtypeStru...]
where the time goes in v5:
time: 86.4 us; the launch traced here: 85.4 us
  Pallas kernels  84.7 us (98%)
    pallas_call x1, Pallas kernels, whole(): pl.pallas_call(functools.partial(kernel, factor), out_shape=[jax.ShapeDty...  81.4 us
    pallas_call x1, Pallas kernels, hand_over(): pl.pallas_call(hand_over_kernel, grid=(4,), out_shape=[jax.ShapeDtypeStru...  3.31 us

profile of v5, /device:TPU:1, one launch (start us, length us, event | category | flops | bytes accessed | tf_op | source)
XLA Modules:
  0.0 85.4 jit_solution(1368192457734932752)
XLA Ops:
  0.6 81.4 %shard_map.129 = (bf16[8,3,16,1024]{3,2,1,0:T(8,128)(2,1)}, f32[8,1024]{1,0:T(8,128)}, f32[8,1024]{1,0:T(8,128)}, f32[8,1024]{1,0:T(8,128)}) custom-call(bf16[2,13,64,1024]{3,2,1,0:T(8,128)(2,1)} %bitcast.4, bf16[2,3,64,1024]{3,2,1,0:T(8,128)(2,1)} %bitcast.5, bf16[1024,1024]{1,0:T(8,128)(2,1)} %kw_far.1, bf16[1024,1024]{1,0:T(8,128)(2,1)} %vw_far.1, ...), custom_call_target="tpu_custom_call" | custom-call | tf_op jit(solution)/shard_map/pallas_call | solution.py:754
  82.1 3.3 %shard_map.130 = (bf16[8,3,16,1024]{3,2,1,0:T(8,128)(2,1)}, f32[8,1024]{1,0:T(8,128)}, f32[8,1024]{1,0:T(8,128)}, f32[8,1024]{1,0:T(8,128)}) custom-call(bf16[8,3,16,1024]{3,2,1,0:T(8,128)(2,1)} %get-tuple-element.12.tile, f32[8,1024]{1,0:T(8,128)} %get-tuple-element.13.refs_0_, f32[8,1024]{1,0:T(8,128)} %get-tuple-element.14.refs_1_, ...), custom_call_target="tpu_custom_call" | custom-call | tf_op jit(solution)/shard_map/pallas_call | solution.py:788

commit v6 on v4

--- a/solution.py
+++ b/solution.py
@@ -59,7 +59,7 @@
     others += [((lat + step) % 32, (lon + turn) % 4) for step, turn in ((1, 0), (31, 0), (1, 1), (31, 3))]
     for other in others:
         pl.semaphore_signal(barrier, inc=1, device_id=other, device_id_type=MESH)
-    pl.semaphore_wait(barrier, len(others))
+    return lambda: pl.semaphore_wait(barrier, len(others))
 
 
 PARTS = (
@@ -605,11 +605,13 @@
 
 
 def kernel(factor, tokens, grads, kw_far, vw_far, ro_far, lq, gains, qkv, ow, label, *refs):
-    out, grad_key, grad_value, grad_out = refs[:4]
+    out_far, grad_key, grad_value, grad_out = refs[:4]
     w, latents, x, rows_out, columns_out, rows_in, columns_in, corner_in = refs[4:12]
     packed, landing = refs[12:15], refs[15:45]
-    g_send, g_recv, r_send, r_recv, t_send, t_recv, e_send, e_recv, near = refs[45:]
+    g_send, g_recv, r_send, r_recv, t_send, t_recv, e_send, e_recv, near, out = refs[45:]
+    leave = pltpu.make_async_copy(out, out_far, near.at[14])
     place = my_place()
+    all_greeted = greet(place)
     y = place["y"]
     own = []
     for layer in range(2):
@@ -658,7 +660,7 @@
         copies = [pltpu.make_async_copy(far, here, near.at[9 + i]) for i, (far, here) in enumerate(pairs)]
         for copy in copies:
             copy.start()
-        greet(place)
+        all_greeted()
         for copy in own:
             copy.wait()
         gathered(0, 0)()
@@ -724,6 +726,7 @@
         reduced(2, 2)()
         hooks = {1: both(gathered(1, 5), reduced(3, 0, 1)), 2: reduced(3, 2)}
         second_sublayer(core, middle, gains[1:2, :], w, normed, mixed, bias, out, hooks)
+        leave.start()
         reduced(4, 0, 1, 2)()
         edges.drain()
 
@@ -735,6 +738,7 @@
         pltpu.VMEM((4, 96, 96), F32),
     )
     finish_gradients(factor, [part.result() for part in sums], lq, grad_key, grad_value, grad_out)
+    leave.wait()
     tiles.drain()
     for part in layers[0] + layers[1] + sums:
         part.drain()
@@ -750,7 +754,7 @@
         functools.partial(kernel, factor),
         out_shape=[jax.ShapeDtypeStruct((8, LATENT, 16, D), BF16)] + [jax.ShapeDtypeStruct((8, D), F32)] * 3,
         in_specs=[far] * 5 + [vmem, vmem, far, far, vmem],
-        out_specs=[vmem] * 4,
+        out_specs=[far] + [vmem] * 3,
         scratch_shapes=[
             pltpu.VMEM((16, 2, 2, 4, 2, 4, 32, 128), BF16),
             pltpu.VMEM((2, LATENT, 64, D), BF16),
@@ -764,7 +768,7 @@
         + [pltpu.VMEM((2, 4, 2, 4, 2, 16, width), BF16) for width in WIDTHS]
         + landings
         + [dma((6, 16)), dma((6, 16)), dma((3, 10)), dma((3, 10))]
-        + [dma((3,)), dma((3,)), dma((3,)), dma((3,)), dma((14,))],
+        + [dma((3,)), dma((3,)), dma((3,)), dma((3,)), dma((15,)), pltpu.VMEM((8, LATENT, 16, D), BF16)],
         compiler_params=pltpu.CompilerParams(collective_id=0, has_side_effects=True, vmem_limit_bytes=63 * MIB),
     )(tokens, grads, kw, vw, ro, lq, gains, qkv, ow, label)
 

time: 83.9 us -> 83.6 us (level)
  no operation moved by 1% of the time
where the time goes in v6:
time: 83.6 us; the launch traced here: 83.4 us
  Pallas kernels  82.8 us (99%)
    pallas_call x1, Pallas kernels, whole(): pl.pallas_call(functools.partial(kernel, factor), out_shape=[jax.ShapeDty...  80.7 us
    pallas_call x1, Pallas kernels, hand_over(): pl.pallas_call(hand_over_kernel, out_shape=[jax.ShapeDtypeStruct(r.shape,...  2.1 us

profile of v6, /device:TPU:1, one launch (start us, length us, event | category | flops | bytes accessed | tf_op | source)
XLA Modules:
  0.0 83.4 jit_solution(6657779912576467414)
XLA Ops:
  0.6 80.7 %shard_map.129 = (bf16[8,3,16,1024]{3,2,1,0:T(8,128)(2,1)}, f32[8,1024]{1,0:T(8,128)}, f32[8,1024]{1,0:T(8,128)}, f32[8,1024]{1,0:T(8,128)}) custom-call(bf16[2,13,64,1024]{3,2,1,0:T(8,128)(2,1)} %bitcast.4, bf16[2,3,64,1024]{3,2,1,0:T(8,128)(2,1)} %bitcast.5, bf16[1024,1024]{1,0:T(8,128)(2,1)} %kw_far.1, bf16[1024,1024]{1,0:T(8,128)(2,1)} %vw_far.1, ...), custom_call_target="tpu_custom_call" | custom-call | tf_op jit(solution)/shard_map/pallas_call | solution.py:753
  81.3 2.1 %shard_map.130 = (bf16[8,3,16,1024]{3,2,1,0:T(8,128)(2,1)}, f32[8,1024]{1,0:T(8,128)}, f32[8,1024]{1,0:T(8,128)}, f32[8,1024]{1,0:T(8,128)}) custom-call(bf16[8,3,16,1024]{3,2,1,0:T(8,128)(2,1)} %get-tuple-element.12.refs_0_, f32[8,1024]{1,0:T(8,128)} %get-tuple-element.13.refs_1_, f32[8,1024]{1,0:T(8,128)} %get-tuple-element.14.refs_2_, ...), custom_call_target="tpu_custom_call" | custom-call | tf_op jit(solution)/shard_map/pallas_call | solution.py:783

commit v7 on v6

--- a/solution.py
+++ b/solution.py
@@ -103,16 +103,20 @@
         if phase < 2:
             return self.copy(4 * phase + k, self.region(phase, me), moved(self.place, dim, (1, -1, 2)[k]))
         other = moved(self.place, dim, 1 if k % 2 == 0 else -1)
-        if k < 2:
-            return self.copy(4 * phase + k, self.region(phase, me), other)
-        return self.copy(4 * phase + k, self.region(phase, (me + 7 - 2 * k) % 4, k - 2), other)
+        source = (me + (0, 0, 3, 1, 0, 0)[k]) % 4
+        return self.copy(self.slot(k), self.region(2, source, (0, 1, 0, 1, 1, 0)[k]), other)
+
+    def slot(self, k):
+        return 8 + k if k < 4 else 12 + k
 
     def arrival(self, phase, k):
         dim = self.order[phase]
         me = self.place[dim]
-        source = (me + (3, 1, 2, 2)[k]) % 4
-        half = k - 2 if phase == 2 and k > 1 else None
-        return self.copy(4 * phase + k, self.region(phase, source, half), moved(self.place, dim, 1))
+        other = moved(self.place, dim, 1)
+        source = (me + (3, 1, 2, 2, 3, 1)[k]) % 4
+        if phase < 2:
+            return self.copy(4 * phase + k, self.region(phase, source), other)
+        return self.copy(self.slot(k), self.region(2, source, (0, 1, 0, 1, 1, 0)[k]), other)
 
     def across(self, k, core):
         ref = self.region(2, (self.place[self.order[2]] + (0, 3, 1, 2)[k]) % 4, None, core)
@@ -124,7 +128,7 @@
             if s > 0:
                 for k in range(3):
                     self.arrival(s - 1, k).wait_recv()
-            for k in range(3 if s < 2 else 2):
+            for k in range(3) if s < 2 else (0, 1, 4, 5):
                 self.ring(s, k).start()
             if s == 2:
                 self.across(0, core).start()
@@ -132,8 +136,11 @@
             for k in range(2):
                 self.arrival(2, k).wait_recv()
                 self.ring(2, k + 2).start()
+        elif s == 4:
+            for k in range(2):
+                self.arrival(2, k + 4).wait_recv()
                 self.across(k + 1, core).start()
-        elif s == 4:
+        elif s == 5:
             for k in (2, 3):
                 self.arrival(2, k).wait_recv()
             self.across(3, core).start()
@@ -143,7 +150,7 @@
 
     def drain(self):
         for phase in range(3):
-            for k in range(3 if phase < 2 else 4):
+            for k in range(3 if phase < 2 else 6):
                 self.ring(phase, k).wait_send()
         for k in range(4):
             self.across(k, self.place["core"]).wait_send()
@@ -688,7 +695,7 @@
         tiles.start(True)
         out_gradient(grad, att, turned, packed[2])
         reduced(0, 2)()
-        token_gradients(tok, values, d_logits, turned, packed, {})
+        token_gradients(tok, values, d_logits, turned, packed, {0: gathered(0, 4)})
 
     pl.run_scoped(
         resampler,
@@ -716,15 +723,15 @@
         label_mask(label, place, bias)
         reduced(1, 1)()
         tiles.finish()
-        ready = both(gathered(0, 4), reduced(1, 0))
-        hooks = {1: gathered(0, 5), 2: gathered(1, 3)}
+        ready = both(gathered(0, 5), reduced(1, 0))
+        hooks = {1: gathered(0, 6), 2: gathered(1, 3), 3: gathered(1, 4)}
         first_sublayer(core, x, gains[0:1, :], w, normed, mixed, middle, ready, hooks)
         edges.start()
-        gathered(1, 4)()
+        gathered(1, 5)()
         reduced(2, 0, 1)()
         edges.finish()
         reduced(2, 2)()
-        hooks = {1: both(gathered(1, 5), reduced(3, 0, 1)), 2: reduced(3, 2)}
+        hooks = {1: both(gathered(1, 6), reduced(3, 0, 1)), 2: reduced(3, 2)}
         second_sublayer(core, middle, gains[1:2, :], w, normed, mixed, bias, out, hooks)
         leave.start()
         reduced(4, 0, 1, 2)()
@@ -767,7 +774,7 @@
         ]
         + [pltpu.VMEM((2, 4, 2, 4, 2, 16, width), BF16) for width in WIDTHS]
         + landings
-        + [dma((6, 16)), dma((6, 16)), dma((3, 10)), dma((3, 10))]
+        + [dma((6, 18)), dma((6, 18)), dma((3, 10)), dma((3, 10))]
         + [dma((3,)), dma((3,)), dma((3,)), dma((3,)), dma((15,)), pltpu.VMEM((8, LATENT, 16, D), BF16)],
         compiler_params=pltpu.CompilerParams(collective_id=0, has_side_effects=True, vmem_limit_bytes=63 * MIB),
     )(tokens, grads, kw, vw, ro, lq, gains, qkv, ow, label)

time: 83.6 us -> 84.6 us (1.012)
  Pallas kernels: 82.8 us -> 83.8 us
    pallas_call x1, Pallas kernels: 80.7 us -> 81.7 us  [whole(): pl.pallas_call(functools.partial(kernel, factor), out_shape=[jax.ShapeDty...]
where the time goes in v7:
time: 84.6 us; the launch traced here: 84.4 us
  Pallas kernels  83.8 us (99%)
    pallas_call x1, Pallas kernels, whole(): pl.pallas_call(functools.partial(kernel, factor), out_shape=[jax.ShapeDty...  81.7 us
    pallas_call x1, Pallas kernels, hand_over(): pl.pallas_call(hand_over_kernel, out_shape=[jax.ShapeDtypeStruct(r.shape,...  2.1 us

profile of v7, /device:TPU:1, one launch (start us, length us, event | category | flops | bytes accessed | tf_op | source)
XLA Modules:
  0.0 84.4 jit_solution(387920371557765057)
XLA Ops:
  0.6 81.7 %shard_map.129 = (bf16[8,3,16,1024]{3,2,1,0:T(8,128)(2,1)}, f32[8,1024]{1,0:T(8,128)}, f32[8,1024]{1,0:T(8,128)}, f32[8,1024]{1,0:T(8,128)}) custom-call(bf16[2,13,64,1024]{3,2,1,0:T(8,128)(2,1)} %bitcast.4, bf16[2,3,64,1024]{3,2,1,0:T(8,128)(2,1)} %bitcast.5, bf16[1024,1024]{1,0:T(8,128)(2,1)} %kw_far.1, bf16[1024,1024]{1,0:T(8,128)(2,1)} %vw_far.1, ...), custom_call_target="tpu_custom_call" | custom-call | tf_op jit(solution)/shard_map/pallas_call | solution.py:760
  82.3 2.1 %shard_map.130 = (bf16[8,3,16,1024]{3,2,1,0:T(8,128)(2,1)}, f32[8,1024]{1,0:T(8,128)}, f32[8,1024]{1,0:T(8,128)}, f32[8,1024]{1,0:T(8,128)}) custom-call(bf16[8,3,16,1024]{3,2,1,0:T(8,128)(2,1)} %get-tuple-element.12.refs_0_, f32[8,1024]{1,0:T(8,128)} %get-tuple-element.13.refs_1_, f32[8,1024]{1,0:T(8,128)} %get-tuple-element.14.refs_2_, ...), custom_call_target="tpu_custom_call" | custom-call | tf_op jit(solution)/shard_map/pallas_call | solution.py:790
